TPU v7x, 128 devices: a whole 4x4x4 slice. The times are simulated.
128 devices in a mesh: rep: 2 (over z_hi), section: 8 (over x, core), tp: 8 (over y, z_lo).
Axes of the slice: x: 4, y: 4, z: 4 (z_hi: 2, z_lo: 2; z = z_hi * 2 + z_lo), core: 2. Of those that a mesh axis runs over, the one named last changes fastest.
Arguments:
- section_map: int32 [2, 8], replicated, may hold values from 0 to 7, as said below
- checkpoint: bfloat16 [2, 8, 2, 64, 4096], P('rep', 'section'), may hold values from -6 to 6
- top_grad: bfloat16 [2, 2, 64, 4096], P('rep'), may hold values from -6 to 6
- value_weight: bfloat16 [2, 16, 4096, 4096], P('rep', 'section', None, 'tp'), may hold values from -0.09375 to 0.09375
- out_weight: bfloat16 [2, 16, 4096, 4096], P('rep', 'section', None, 'tp'), may hold values from -0.09375 to 0.09375
Outputs:
- value_grad: bfloat16 [8, 4096, 4096], P(None, ('rep', 'section'), 'tp')
- out_grad: bfloat16 [8, 4096, 4096], P(None, ('rep', 'section'), 'tp')
Inputs may be any that keep to these rules, and one draw needn't show every extreme that they name: `section_map`: row r lists the section of each layer for replica r; entries never fall along a row; a section holds at most 2 layers and may hold none.
All inputs are finite; a program needn't handle non-finite values.
Results may differ from a plain program's by a relative error of at most 0.035.
Values may be sent and summed in bfloat16 or wider, within the bound.
No kernel may reach another device: no remote copies, remote signals or barrier semaphores. Data moves between devices by JAX's collectives and lax.ppermute only.
A program may use at most 192 MiB of HBM per device.

v0:
```python
import jax
import jax.numpy as jnp
from jax import lax
from jax.sharding import PartitionSpec as P


def passed_along(block, axis, distance):
    devices = range(lax.axis_size(axis))
    route = [(i - distance, i) for i in devices if i - distance in devices]
    return lax.ppermute(block, axis, route)


def silu_slope(preact):
    sigma = jax.nn.sigmoid(preact)
    return sigma * (1.0 + preact * (1.0 - sigma))


def add_heads(base, term):
    summed = lax.psum(term.astype(jnp.bfloat16), "tp").astype(jnp.float32)
    return (base.astype(jnp.float32) + summed).astype(jnp.bfloat16)


def slot_tables(section_rows, section_total, slot_total, layer_total):
    section_ids = jnp.arange(section_total, dtype=jnp.int32)
    slot_ids = jnp.arange(slot_total, dtype=jnp.int32)
    layer_ids = jnp.arange(layer_total, dtype=jnp.int32)
    section_counts = jnp.sum(
        (section_rows[:, None, :] == section_ids[None, :, None]).astype(jnp.int32), axis=2
    )
    first_layers = jnp.sum(
        (section_rows[:, None, :] < section_ids[None, :, None]).astype(jnp.int32), axis=2
    )
    layer_of = first_layers[:, :, None] + slot_ids[None, None, :]
    is_valid = slot_ids[None, None, :] < section_counts[:, :, None]
    return ((layer_of[..., None] == layer_ids) & is_valid[..., None]).astype(jnp.bfloat16)


def per_device(section_map, checkpoint, top_grad, value_weight, out_weight):
    slot_total = value_weight.shape[1]
    section_total = lax.axis_size("section")
    replica_total = lax.axis_size("rep")
    my_section = lax.axis_index("section")
    my_replica = lax.axis_index("rep")
    layer_total = section_map.shape[1]
    own_map = lax.dynamic_index_in_dim(section_map, my_replica, 0, keepdims=False)
    section_count = jnp.sum((own_map == my_section).astype(jnp.int32))
    micro_count, token_count, model_width = (
        checkpoint.shape[2],
        checkpoint.shape[3],
        checkpoint.shape[4],
    )
    head_width = value_weight.shape[3]
    row_count = micro_count * token_count
    contract_last = (((1,), (1,)), ((), ()))
    contract_first = (((0,), (0,)), ((), ()))
    current = checkpoint[0, 0].reshape(row_count, model_width)
    slot_inputs, slot_preacts, slot_acts = ([], [], [])
    for slot_index in range(slot_total):
        preact = jnp.dot(current, value_weight[0, slot_index], preferred_element_type=jnp.float32)
        activated = jax.nn.silu(preact).astype(jnp.bfloat16)
        slot_inputs.append(current)
        slot_preacts.append(preact.reshape(micro_count, token_count, head_width))
        slot_acts.append(activated)
        projected = lax.dot_general(
            activated, out_weight[0, slot_index], contract_last, preferred_element_type=jnp.float32
        )
        advanced = add_heads(current, projected)
        current = jnp.where(slot_index < section_count, advanced, current)
    preact_all = jnp.stack(slot_preacts)

    def one_turn(turn_index, carry):
        incoming, grad_store, head_store = carry
        micro_now = turn_index - (section_total - 1 - my_section)
        active = (micro_now >= 0) & (micro_now < micro_count)
        micro_index = jnp.clip(micro_now, 0, micro_count - 1)
        top_slice = lax.dynamic_index_in_dim(top_grad[0], micro_index, 0, keepdims=False)
        upstream = jnp.where(my_section == section_total - 1, top_slice, incoming)
        for slot_index in reversed(range(slot_total)):
            preact = lax.dynamic_index_in_dim(
                preact_all[slot_index], micro_index, 0, keepdims=False
            )
            act_grad = jnp.dot(
                upstream, out_weight[0, slot_index], preferred_element_type=jnp.float32
            )
            head_grad = (act_grad * silu_slope(preact)).astype(jnp.bfloat16)
            old_grad = grad_store[slot_index, micro_index]
            grad_store = grad_store.at[slot_index, micro_index].set(
                jnp.where(active, upstream, old_grad)
            )
            old_head = head_store[slot_index, micro_index]
            head_store = head_store.at[slot_index, micro_index].set(
                jnp.where(active, head_grad, old_head)
            )
            term = lax.dot_general(
                head_grad,
                value_weight[0, slot_index],
                contract_last,
                preferred_element_type=jnp.float32,
            )
            advanced = add_heads(upstream, term)
            upstream = jnp.where(slot_index < section_count, advanced, upstream)
        incoming = passed_along(upstream, "section", -1)
        return (incoming, grad_store, head_store)

    start = (
        jnp.zeros((token_count, model_width), jnp.bfloat16),
        jnp.zeros((slot_total, micro_count, token_count, model_width), jnp.bfloat16),
        jnp.zeros((slot_total, micro_count, token_count, head_width), jnp.bfloat16),
    )
    _, grad_store, head_store = lax.fori_loop(0, section_total + micro_count - 1, one_turn, start)
    parts = replica_total * section_total
    piece = model_width // parts
    value_terms, out_terms = ([], [])
    for slot_index in range(slot_total):
        grad_rows = grad_store[slot_index].reshape(row_count, model_width)
        head_rows = head_store[slot_index].reshape(row_count, head_width)
        out_terms.append(
            lax.dot_general(
                grad_rows, slot_acts[slot_index], contract_first, preferred_element_type=jnp.float32
            ).astype(jnp.bfloat16)
        )
        value_terms.append(
            lax.dot_general(
                slot_inputs[slot_index],
                head_rows,
                contract_first,
                preferred_element_type=jnp.float32,
            ).astype(jnp.bfloat16)
        )
    grads = jnp.stack([jnp.stack(value_terms), jnp.stack(out_terms)])
    spread = grads.reshape(2, slot_total, parts, piece, head_width)
    received = lax.all_to_all(spread, ("rep", "section"), split_axis=2, concat_axis=2, tiled=True)
    received = received.reshape(2, slot_total, replica_total, section_total, piece, head_width)
    table = slot_tables(section_map, section_total, slot_total, layer_total)
    summed = jnp.einsum("rskl,mkrsch->mlch", table, received, preferred_element_type=jnp.float32)
    result = summed.astype(jnp.bfloat16)
    return (result[0], result[1])


def solution(mesh):
    placed = (
        P(),
        P("rep", "section", None, None, None),
        P("rep", None, None, None),
        P("rep", "section", None, "tp"),
        P("rep", "section", None, "tp"),
    )
    return jax.shard_map(
        per_device,
        mesh=mesh,
        in_specs=placed,
        out_specs=(P(None, ("rep", "section"), "tp"), P(None, ("rep", "section"), "tp")),
        check_vma=False,
    )
```

profile of v0, /device:TPU:1, one launch (start us, length us, event | category | flops | bytes accessed | tf_op | source)
XLA Modules:
  0.0 2065.6 jit_solution(474806581503669465)
XLA Ops:
  17.2 75.1 %all-reduce.4.cloned.1.call-done = bf16[128,4096]{1,0:T(8,128)(2,1)} async-done(((bf16[128,4096]{1,0:T(8,128)(2,1)}), bf16[128,4096]{1,0:T(8,128)(2,1)}) %all-reduce.4.cloned.1.call-update) | async-done | bytes 1048592 | tf_op jit(solution)/shard_map/psum | solution.py:19
  97.4 1648.2 %while.23 = (s32[]{:T(128)}, bf16[64,4096]{1,0:T(8,128)(2,1)}, bf16[2,2,64,4096]{3,2,1,0:T(8,128)(2,1)S(1)}, bf16[2,2,64,512]{3,2,1,0:T(8,128)(2,1)S(1)}, pred[]...) while((s32[]{:T(128)}, bf16[64,4096]{1,0:T(8,128)(2,1)}, ...), condition=%wide.region_7.8_spmd, body=%wide.region_2.7_spmd.sunk | while | flops 1079443456 | bytes 89657352 | solution.py:110
  108.8 72.3 %all-reduce.6.cloned.1.call-done = bf16[64,4096]{1,0:T(8,128)(2,1)} async-done(((bf16[64,4096]{1,0:T(8,128)(2,1)}), bf16[64,4096]{1,0:T(8,128)(2,1)}) %all-reduce.6.cloned.1.call-update) | async-done | bytes 524304 | tf_op jit(solution)/shard_map/while/body/eval_jaxpr/psum | solution.py:19
  192.3 74.3 %all-reduce.8.cloned.1.call-done = bf16[64,4096]{1,0:T(8,128)(2,1)} async-done(((bf16[64,4096]{1,0:T(8,128)(2,1)}), bf16[64,4096]{1,0:T(8,128)(2,1)}) %all-reduce.8.cloned.1.call-update) | async-done | bytes 524304 | tf_op jit(solution)/shard_map/while/body/eval_jaxpr/psum | solution.py:19
  276.4 8.1 collective-permute-done
  296.7 67.0 %all-reduce.6.cloned.1.call-done = bf16[64,4096]{1,0:T(8,128)(2,1)} async-done(((bf16[64,4096]{1,0:T(8,128)(2,1)}), bf16[64,4096]{1,0:T(8,128)(2,1)}) %all-reduce.6.cloned.1.call-update) | async-done | bytes 524304 | tf_op jit(solution)/shard_map/while/body/eval_jaxpr/psum | solution.py:19
  374.8 74.3 %all-reduce.8.cloned.1.call-done = bf16[64,4096]{1,0:T(8,128)(2,1)} async-done(((bf16[64,4096]{1,0:T(8,128)(2,1)}), bf16[64,4096]{1,0:T(8,128)(2,1)}) %all-reduce.8.cloned.1.call-update) | async-done | bytes 524304 | tf_op jit(solution)/shard_map/while/body/eval_jaxpr/psum | solution.py:19
  479.2 67.0 %all-reduce.6.cloned.1.call-done = bf16[64,4096]{1,0:T(8,128)(2,1)} async-done(((bf16[64,4096]{1,0:T(8,128)(2,1)}), bf16[64,4096]{1,0:T(8,128)(2,1)}) %all-reduce.6.cloned.1.call-update) | async-done | bytes 524304 | tf_op jit(solution)/shard_map/while/body/eval_jaxpr/psum | solution.py:19
  557.3 74.3 %all-reduce.8.cloned.1.call-done = bf16[64,4096]{1,0:T(8,128)(2,1)} async-done(((bf16[64,4096]{1,0:T(8,128)(2,1)}), bf16[64,4096]{1,0:T(8,128)(2,1)}) %all-reduce.8.cloned.1.call-update) | async-done | bytes 524304 | tf_op jit(solution)/shard_map/while/body/eval_jaxpr/psum | solution.py:19
  661.8 67.0 %all-reduce.6.cloned.1.call-done = bf16[64,4096]{1,0:T(8,128)(2,1)} async-done(((bf16[64,4096]{1,0:T(8,128)(2,1)}), bf16[64,4096]{1,0:T(8,128)(2,1)}) %all-reduce.6.cloned.1.call-update) | async-done | bytes 524304 | tf_op jit(solution)/shard_map/while/body/eval_jaxpr/psum | solution.py:19
  739.9 74.2 %all-reduce.8.cloned.1.call-done = bf16[64,4096]{1,0:T(8,128)(2,1)} async-done(((bf16[64,4096]{1,0:T(8,128)(2,1)}), bf16[64,4096]{1,0:T(8,128)(2,1)}) %all-reduce.8.cloned.1.call-update) | async-done | bytes 524304 | tf_op jit(solution)/shard_map/while/body/eval_jaxpr/psum | solution.py:19
  844.2 67.0 %all-reduce.6.cloned.1.call-done = bf16[64,4096]{1,0:T(8,128)(2,1)} async-done(((bf16[64,4096]{1,0:T(8,128)(2,1)}), bf16[64,4096]{1,0:T(8,128)(2,1)}) %all-reduce.6.cloned.1.call-update) | async-done | bytes 524304 | tf_op jit(solution)/shard_map/while/body/eval_jaxpr/psum | solution.py:19
  922.4 74.3 %all-reduce.8.cloned.1.call-done = bf16[64,4096]{1,0:T(8,128)(2,1)} async-done(((bf16[64,4096]{1,0:T(8,128)(2,1)}), bf16[64,4096]{1,0:T(8,128)(2,1)}) %all-reduce.8.cloned.1.call-update) | async-done | bytes 524304 | tf_op jit(solution)/shard_map/while/body/eval_jaxpr/psum | solution.py:19
  1006.6 8.1 collective-permute-done
  1026.9 67.0 %all-reduce.6.cloned.1.call-done = bf16[64,4096]{1,0:T(8,128)(2,1)} async-done(((bf16[64,4096]{1,0:T(8,128)(2,1)}), bf16[64,4096]{1,0:T(8,128)(2,1)}) %all-reduce.6.cloned.1.call-update) | async-done | bytes 524304 | tf_op jit(solution)/shard_map/while/body/eval_jaxpr/psum | solution.py:19
  1104.9 74.2 %all-reduce.8.cloned.1.call-done = bf16[64,4096]{1,0:T(8,128)(2,1)} async-done(((bf16[64,4096]{1,0:T(8,128)(2,1)}), bf16[64,4096]{1,0:T(8,128)(2,1)}) %all-reduce.8.cloned.1.call-update) | async-done | bytes 524304 | tf_op jit(solution)/shard_map/while/body/eval_jaxpr/psum | solution.py:19
  1209.3 67.0 %all-reduce.6.cloned.1.call-done = bf16[64,4096]{1,0:T(8,128)(2,1)} async-done(((bf16[64,4096]{1,0:T(8,128)(2,1)}), bf16[64,4096]{1,0:T(8,128)(2,1)}) %all-reduce.6.cloned.1.call-update) | async-done | bytes 524304 | tf_op jit(solution)/shard_map/while/body/eval_jaxpr/psum | solution.py:19
  1287.4 74.3 %all-reduce.8.cloned.1.call-done = bf16[64,4096]{1,0:T(8,128)(2,1)} async-done(((bf16[64,4096]{1,0:T(8,128)(2,1)}), bf16[64,4096]{1,0:T(8,128)(2,1)}) %all-reduce.8.cloned.1.call-update) | async-done | bytes 524304 | tf_op jit(solution)/shard_map/while/body/eval_jaxpr/psum | solution.py:19
  1391.9 67.0 %all-reduce.6.cloned.1.call-done = bf16[64,4096]{1,0:T(8,128)(2,1)} async-done(((bf16[64,4096]{1,0:T(8,128)(2,1)}), bf16[64,4096]{1,0:T(8,128)(2,1)}) %all-reduce.6.cloned.1.call-update) | async-done | bytes 524304 | tf_op jit(solution)/shard_map/while/body/eval_jaxpr/psum | solution.py:19
  1470.0 74.2 %all-reduce.8.cloned.1.call-done = bf16[64,4096]{1,0:T(8,128)(2,1)} async-done(((bf16[64,4096]{1,0:T(8,128)(2,1)}), bf16[64,4096]{1,0:T(8,128)(2,1)}) %all-reduce.8.cloned.1.call-update) | async-done | bytes 524304 | tf_op jit(solution)/shard_map/while/body/eval_jaxpr/psum | solution.py:19
  1574.3 67.0 %all-reduce.6.cloned.1.call-done = bf16[64,4096]{1,0:T(8,128)(2,1)} async-done(((bf16[64,4096]{1,0:T(8,128)(2,1)}), bf16[64,4096]{1,0:T(8,128)(2,1)}) %all-reduce.6.cloned.1.call-update) | async-done | bytes 524304 | tf_op jit(solution)/shard_map/while/body/eval_jaxpr/psum | solution.py:19
  1652.5 74.3 %all-reduce.8.cloned.1.call-done = bf16[64,4096]{1,0:T(8,128)(2,1)} async-done(((bf16[64,4096]{1,0:T(8,128)(2,1)}), bf16[64,4096]{1,0:T(8,128)(2,1)}) %all-reduce.8.cloned.1.call-update) | async-done | bytes 524304 | tf_op jit(solution)/shard_map/while/body/eval_jaxpr/psum | solution.py:19
  1795.2 224.3 %all-to-all-done = bf16[2,2,16,256,512]{3,4,1,0,2:T(8,128)(2,1)} async-done(((bf16[2,2,16,256,512]{3,4,1,0,2:T(8,128)(2,1)}), bf16[2,2,16,256,512]{3,4,1,0,2:T(8,128)(2,1)}, u32[]{:S(2)}, u32[]{:S(2)}) %all-to-all-start) | async-done | bytes 16777248 | tf_op jit(solution)/shard_map/all_to_all | solution.py:132
  2019.5 28.1 %copy.24 = bf16[2,2,16,256,512]{4,2,1,3,0:T(8,128)(2,1)} copy(bf16[2,2,16,256,512]{3,4,1,0,2:T(8,128)(2,1)} %all-to-all-done) | data formatting | bytes 33554432 | tf_op jit(solution)/shard_map/all_to_all | solution.py:132
  (283 shorter events, 428.3 us)
Async XLA Ops:
  7.2 85.2 %all-reduce.4.cloned.1.call-start = ((), (), s32[]{:S(2)}) async-start(), calls=%async_computation.1 | async-start | bytes 2097152 | tf_op jit(solution)/shard_map/psum | solution.py:19
  97.4 83.7 %all-reduce.6.cloned.1.call-start = ((), (), s32[]{:S(2)}) async-start(), calls=%async_computation.2 | async-start | bytes 1048576 | tf_op jit(solution)/shard_map/while/body/eval_jaxpr/psum | solution.py:19
  107.7 158.8 %all-reduce.8.cloned.1.call-start = ((), (), s32[]{:S(2)}) async-start(), calls=%async_computation.3 | async-start | bytes 1048576 | tf_op jit(solution)/shard_map/while/body/eval_jaxpr/psum | solution.py:19
  268.5 16.0 collective-permute-start
  285.3 78.4 %all-reduce.6.cloned.1.call-start = ((), (), s32[]{:S(2)}) async-start(), calls=%async_computation.2 | async-start | bytes 1048576 | tf_op jit(solution)/shard_map/while/body/eval_jaxpr/psum | solution.py:19
  295.5 153.6 %all-reduce.8.cloned.1.call-start = ((), (), s32[]{:S(2)}) async-start(), calls=%async_computation.3 | async-start | bytes 1048576 | tf_op jit(solution)/shard_map/while/body/eval_jaxpr/psum | solution.py:19
  451.1 16.0 collective-permute-start
  467.9 78.4 %all-reduce.6.cloned.1.call-start = ((), (), s32[]{:S(2)}) async-start(), calls=%async_computation.2 | async-start | bytes 1048576 | tf_op jit(solution)/shard_map/while/body/eval_jaxpr/psum | solution.py:19
  478.0 153.6 %all-reduce.8.cloned.1.call-start = ((), (), s32[]{:S(2)}) async-start(), calls=%async_computation.3 | async-start | bytes 1048576 | tf_op jit(solution)/shard_map/while/body/eval_jaxpr/psum | solution.py:19
  650.5 78.3 %all-reduce.6.cloned.1.call-start = ((), (), s32[]{:S(2)}) async-start(), calls=%async_computation.2 | async-start | bytes 1048576 | tf_op jit(solution)/shard_map/while/body/eval_jaxpr/psum | solution.py:19
  660.6 153.5 %all-reduce.8.cloned.1.call-start = ((), (), s32[]{:S(2)}) async-start(), calls=%async_computation.3 | async-start | bytes 1048576 | tf_op jit(solution)/shard_map/while/body/eval_jaxpr/psum | solution.py:19
  832.9 78.4 %all-reduce.6.cloned.1.call-start = ((), (), s32[]{:S(2)}) async-start(), calls=%async_computation.2 | async-start | bytes 1048576 | tf_op jit(solution)/shard_map/while/body/eval_jaxpr/psum | solution.py:19
  843.1 153.6 %all-reduce.8.cloned.1.call-start = ((), (), s32[]{:S(2)}) async-start(), calls=%async_computation.3 | async-start | bytes 1048576 | tf_op jit(solution)/shard_map/while/body/eval_jaxpr/psum | solution.py:19
  998.7 16.0 collective-permute-start
  1015.5 78.3 %all-reduce.6.cloned.1.call-start = ((), (), s32[]{:S(2)}) async-start(), calls=%async_computation.2 | async-start | bytes 1048576 | tf_op jit(solution)/shard_map/while/body/eval_jaxpr/psum | solution.py:19
  1025.7 153.5 %all-reduce.8.cloned.1.call-start = ((), (), s32[]{:S(2)}) async-start(), calls=%async_computation.3 | async-start | bytes 1048576 | tf_op jit(solution)/shard_map/while/body/eval_jaxpr/psum | solution.py:19
  1198.0 78.4 %all-reduce.6.cloned.1.call-start = ((), (), s32[]{:S(2)}) async-start(), calls=%async_computation.2 | async-start | bytes 1048576 | tf_op jit(solution)/shard_map/while/body/eval_jaxpr/psum | solution.py:19
  1208.1 153.6 %all-reduce.8.cloned.1.call-start = ((), (), s32[]{:S(2)}) async-start(), calls=%async_computation.3 | async-start | bytes 1048576 | tf_op jit(solution)/shard_map/while/body/eval_jaxpr/psum | solution.py:19
  1380.6 78.3 %all-reduce.6.cloned.1.call-start = ((), (), s32[]{:S(2)}) async-start(), calls=%async_computation.2 | async-start | bytes 1048576 | tf_op jit(solution)/shard_map/while/body/eval_jaxpr/psum | solution.py:19
  1390.7 153.5 %all-reduce.8.cloned.1.call-start = ((), (), s32[]{:S(2)}) async-start(), calls=%async_computation.3 | async-start | bytes 1048576 | tf_op jit(solution)/shard_map/while/body/eval_jaxpr/psum | solution.py:19
  1563.0 78.4 %all-reduce.6.cloned.1.call-start = ((), (), s32[]{:S(2)}) async-start(), calls=%async_computation.2 | async-start | bytes 1048576 | tf_op jit(solution)/shard_map/while/body/eval_jaxpr/psum | solution.py:19
  1573.2 153.6 %all-reduce.8.cloned.1.call-start = ((), (), s32[]{:S(2)}) async-start(), calls=%async_computation.3 | async-start | bytes 1048576 | tf_op jit(solution)/shard_map/while/body/eval_jaxpr/psum | solution.py:19
  1728.8 16.0 collective-permute-start
  1788.7 230.8 %all-to-all-start = ((bf16[2,2,16,256,512]{3,4,1,0,2:T(8,128)(2,1)}), bf16[2,2,16,256,512]{3,4,1,0,2:T(8,128)(2,1)}, u32[]{:S(2)}, u32[]{:S(2)}) async-start(bf16[2,2,16,256,512]{3,4,1,0,2:T(8,128)(2,1)} %maximum_maximum_fusion), calls=%async_computation | async-start | bytes 33554432 | tf_op jit(solution)/shard_map/all_to_all | solution.py:132
  (52 other events, 1370.8 us)
Sparse Core Ops, SparseCore 0:
  15.4 76.9 all-reduce.3
  107.8 73.3 all-reduce.5
  192.4 74.0 all-reduce.7
  295.6 68.0 all-reduce.5
  374.9 74.1 all-reduce.7
  478.2 68.0 all-reduce.5
  557.4 74.1 all-reduce.7
  660.8 67.9 all-reduce.5
  740.0 74.0 all-reduce.7
  843.2 68.0 all-reduce.5
  922.5 74.1 all-reduce.7
  1025.8 67.9 all-reduce.5
  1105.0 74.0 all-reduce.7
  1208.2 68.0 all-reduce.5
  1287.5 74.1 all-reduce.7
  1390.8 67.9 all-reduce.5
  1470.1 74.0 all-reduce.7
  1573.3 68.0 all-reduce.5
  1652.6 74.1 all-reduce.7
where the time goes:
time: 2070 us
  waiting for transfers between devices  1650 us (80%)
  matrix products  166 us (8%)
  other arithmetic  79.4 us (4%)
  starting transfers between devices  77.7 us (4%)
  local copies, waits for them, and re-layouts  76.4 us (4%)
    psum x19, waiting for transfers between devices, add_heads(): summed = lax.psum(term.astype(jnp.bfloat16), 'tp').astype(jnp.float32)  1350 us
    all_to_all x1, waiting for transfers between devices, per_device(): lax.all_to_all(spread, ('rep', 'section'), split_axis=2, concat_axis=2, t...  224 us
    dot_general x18, matrix products, one_turn(): jnp.dot(upstream, out_weight[0, slot_index], preferred_element_type=jnp.f...  75.3 us
    ppermute x9, waiting for transfers between devices, passed_along(): return lax.ppermute(block, axis, route)  73.2 us
    ppermute x9, starting transfers between devices, passed_along(): return lax.ppermute(block, axis, route)  70.9 us
    dot_general x18, matrix products, one_turn(): lax.dot_general(head_grad, value_weight[0, slot_index], contract_last, pr...  60.3 us
    scatter x18, other arithmetic, one_turn(): grad_store.at[slot_index, micro_index]  46.9 us
  transfers between devices with their start and end apart: 29, of which 29 were waited for; matrix products, arithmetic and copies ran while one was open for 1% of the time, Pallas kernels for 0%

commit v1 on v0

v1 whole, which is shorter than its diff:
```python
import functools

import jax
import jax.numpy as jnp
from jax import lax
from jax.experimental import pallas as pl
from jax.experimental.pallas import tpu as pltpu
from jax.sharding import PartitionSpec as P

BF16 = jnp.bfloat16
F32 = jnp.float32
VMEM_BYTES = 48 * 1024 * 1024
NT = (((1,), (1,)), ((), ()))
TN = (((0,), (0,)), ((), ()))


def silu_slope(preact):
    sigma = jax.nn.sigmoid(preact)
    return sigma * (1.0 + preact * (1.0 - sigma))


def weight_copies(pick_ref, own, sibling, buffer, sems, chunks):
    step = buffer.shape[0] // chunks
    slot = pick_ref[1]

    def begin(source):
        for i in range(chunks):
            rows = pl.ds(i * step, step)
            pltpu.make_async_copy(source.at[slot, rows], buffer.at[rows], sems.at[i]).start()

    if sibling is None:
        begin(own)
    else:
        pl.when(pick_ref[0] == 1)(lambda: begin(own))
        pl.when(pick_ref[0] == 0)(lambda: begin(sibling))

    def wait(i):
        rows = pl.ds(i * step, step)
        pltpu.make_async_copy(own.at[slot, rows], buffer.at[rows], sems.at[i]).wait()

    return wait


def first_product(rows_ref, buffer, wait, chunks):
    step = buffer.shape[0] // chunks
    total = None
    for i in range(chunks):
        wait(i)
        part = jnp.dot(rows_ref[i], buffer[i * step : (i + 1) * step, :], preferred_element_type=F32)
        total = part if total is None else total + part
    return total


def second_product(rows, buffer, wait, chunks, out_ref):
    step = buffer.shape[0] // chunks
    for i in range(chunks):
        wait(i)
        part = lax.dot_general(rows, buffer[i * step : (i + 1) * step, :], NT, preferred_element_type=F32)
        out_ref[i] = part.astype(BF16)


def forward_kernel(chunks, pick_ref, x_ref, v_ref, o_ref, part_ref, act_ref, slope_ref, vbuf, obuf, vsem, osem):
    wait_v = weight_copies(pick_ref, v_ref, None, vbuf, vsem, chunks)
    wait_o = weight_copies(pick_ref, o_ref, None, obuf, osem, chunks)
    pre = first_product(x_ref, vbuf, wait_v, chunks)
    act = jax.nn.silu(pre).astype(BF16)
    act_ref[...] = act
    slope_ref[...] = silu_slope(pre)
    second_product(act, obuf, wait_o, chunks, part_ref)


def last_slot_kernel(chunks, pick_ref, x_ref, v_ref, act_ref, slope_ref, vbuf, vsem):
    wait_v = weight_copies(pick_ref, v_ref, None, vbuf, vsem, chunks)
    pre = first_product(x_ref, vbuf, wait_v, chunks)
    act_ref[...] = jax.nn.silu(pre).astype(BF16)
    slope_ref[...] = silu_slope(pre)


def backward_kernel(
    chunks, pick_ref, g_ref, slope_ref, o_own, o_sib, v_own, v_sib, part_ref, head_ref, obuf, vbuf, osem, vsem
):
    wait_o = weight_copies(pick_ref, o_own, o_sib, obuf, osem, chunks)
    wait_v = weight_copies(pick_ref, v_own, v_sib, vbuf, vsem, chunks)
    act_grad = first_product(g_ref, obuf, wait_o, chunks)
    head = (act_grad * slope_ref[0]).astype(BF16)
    head_ref[...] = head
    second_product(head, vbuf, wait_v, chunks, part_ref)


def last_layer_kernel(chunks, pick_ref, g_ref, slope_ref, o_own, o_sib, head_ref, obuf, osem):
    wait_o = weight_copies(pick_ref, o_own, o_sib, obuf, osem, chunks)
    act_grad = first_product(g_ref, obuf, wait_o, chunks)
    head_ref[...] = (act_grad * slope_ref[0]).astype(BF16)


def call(kernel, pick, operands, specs, outs, weight_shape, weights):
    chunks = operands[0].shape[0]
    flops = 2 * operands[0].shape[1] * weight_shape[0] * weight_shape[1] * weights
    scratch = [pltpu.VMEM(weight_shape, BF16)] * weights + [pltpu.SemaphoreType.DMA((chunks,))] * weights
    return pl.pallas_call(
        functools.partial(kernel, chunks),
        out_shape=outs,
        grid_spec=pltpu.PrefetchScalarGridSpec(
            num_scalar_prefetch=1,
            grid=(1,),
            in_specs=specs,
            out_specs=jax.tree.map(lambda o: pl.BlockSpec(o.shape, lambda i, p, n=len(o.shape): (0,) * n), outs),
            scratch_shapes=scratch,
        ),
        compiler_params=pltpu.CompilerParams(vmem_limit_bytes=VMEM_BYTES),
        cost_estimate=pl.CostEstimate(
            flops=flops, bytes_accessed=weights * weight_shape[0] * weight_shape[1] * 2, transcendentals=0
        ),
    )(pick, *operands)


def whole(array):
    return pl.BlockSpec(array.shape, lambda i, p, n=array.ndim: (0,) * n)


ANY = pl.BlockSpec(memory_space=pl.ANY)


def gradient_kernel(tab_ref, x0, x1, h0, h1, g0, g1, a0, a1, value_ref, out_ref):
    def rows(ref):
        return ref[...].reshape(-1, ref.shape[-1])

    def both(left0, right0, left1, right1):
        left = jnp.concatenate([rows(left0), rows(left1)], axis=0)
        right = jnp.concatenate([rows(right0), rows(right1)], axis=0)
        return lax.dot_general(left, right, TN, preferred_element_type=F32).astype(BF16)

    value_ref[0] = both(x0, h0, x1, h1)
    out_ref[0] = both(g0, a0, g1, a1)


def gradients(section_map, position, slot_of, x_all, head_all, g_all, act_all):
    layers = section_map.shape[1]
    table = jnp.stack([section_map, slot_of, position]).astype(jnp.int32)

    def by_slot(r, array):
        return pl.BlockSpec((1, 1, 1) + array.shape[3:], lambda l, t: (r, t[0, r, l], t[1, r, l], 0, 0))

    def by_window(r, array):
        shape = array.shape
        return pl.BlockSpec(
            (1, 1, shape[2], 1) + shape[4:], lambda l, t: (r, t[0, r, l] // 2, 0, t[2, r, l], 0, 0)
        )

    piece, width = x_all.shape[-1], act_all.shape[-1]
    out = jax.ShapeDtypeStruct((layers, piece, width), BF16)
    out_spec = pl.BlockSpec((1, piece, width), lambda l, t: (l, 0, 0))
    return pl.pallas_call(
        gradient_kernel,
        out_shape=(out, out),
        grid_spec=pltpu.PrefetchScalarGridSpec(
            num_scalar_prefetch=1,
            grid=(layers,),
            in_specs=[by_slot(0, x_all), by_slot(1, x_all), by_window(0, head_all), by_window(1, head_all)]
            + [by_window(0, g_all), by_window(1, g_all), by_slot(0, act_all), by_slot(1, act_all)],
            out_specs=(out_spec, out_spec),
        ),
        compiler_params=pltpu.CompilerParams(vmem_limit_bytes=VMEM_BYTES),
    )(table, x_all, x_all, head_all, head_all, g_all, g_all, act_all, act_all)


def per_device(section_map, checkpoint, top_grad, value_weight, out_weight):
    tp_total = lax.axis_size("tp")
    section_total = lax.axis_size("section")
    replica_total = lax.axis_size("rep")
    owners = replica_total * section_total
    rep, section, tp = (lax.axis_index(name) for name in ("rep", "section", "tp"))
    chip, core = section // 2, section % 2
    layers = section_map.shape[1]
    _, _, micro, tokens, model = checkpoint.shape
    slots, width = value_weight.shape[1], value_weight.shape[3]
    rows = micro * tokens
    cut = model // tp_total
    piece = model // owners
    v_own, o_own = value_weight[0], out_weight[0]
    weight_shape = (model, width)

    layer_ids = jnp.arange(layers, dtype=jnp.int32)
    first_of = jnp.sum(section_map[:, None, :] < section_map[:, :, None], axis=2).astype(jnp.int32)
    slot_of = layer_ids[None] - first_of
    chip_of = section_map // 2
    window = 2 * slots
    chip_first = jnp.sum(chip_of[:, None, :] < jnp.arange(section_total // 2)[None, :, None], axis=2)
    window_first = jnp.minimum(chip_first, layers - window).astype(jnp.int32)
    position = layer_ids[None] - jnp.take_along_axis(window_first, chip_of, axis=1)
    my_map = lax.dynamic_index_in_dim(section_map, rep, 0, keepdims=False)
    my_slot = lax.dynamic_index_in_dim(slot_of, rep, 0, keepdims=False)
    my_window = lax.dynamic_index_in_dim(window_first, rep, 0, keepdims=False)[chip]

    swap = [(i, i ^ 1) for i in range(section_total)]
    o_sib = lax.ppermute(o_own, "section", swap)
    v_sib = lax.ppermute(v_own, "section", swap)

    def by_cut(array):
        return array.reshape(-1, tp_total, cut).transpose(1, 0, 2)

    def reduce_slices(parts, base):
        got = lax.all_to_all(parts, "tp", 0, 0, tiled=True)
        mine = lax.dynamic_index_in_dim(base, tp, 0, keepdims=False)
        return (mine.astype(F32) + jnp.sum(got.astype(F32), axis=0)).astype(BF16)

    def gather_slices(mine):
        spread = jnp.broadcast_to(mine[None], (tp_total,) + mine.shape)
        return lax.all_to_all(spread, "tp", 0, 0, tiled=True)

    x_first = by_cut(checkpoint[0, 0].reshape(rows, model))
    wide = jax.ShapeDtypeStruct((rows, width), F32)
    narrow = jax.ShapeDtypeStruct((rows, width), BF16)
    parts, act_first, slope_first = call(
        forward_kernel,
        jnp.array([1, 0], jnp.int32),
        (x_first, v_own, o_own),
        [whole(x_first), ANY, ANY],
        (jax.ShapeDtypeStruct(x_first.shape, BF16), narrow, wide),
        weight_shape,
        2,
    )
    x_second = gather_slices(reduce_slices(parts, x_first))
    act_second, slope_second = call(
        last_slot_kernel,
        jnp.array([1, 1], jnp.int32),
        (x_second, v_own),
        [whole(x_second), ANY],
        (narrow, wide),
        weight_shape,
        1,
    )
    acts = jnp.stack([act_first, act_second])
    act_all = lax.all_gather(acts, ("rep", "section"), axis=0, tiled=False)
    act_all = act_all.reshape(replica_total, section_total, slots, rows, width)
    xs = jnp.stack([x_first, x_second]).reshape(slots, tp_total, rows, 2, piece)
    x_all = lax.all_to_all(
        xs.transpose(1, 3, 0, 2, 4).reshape(owners, slots, rows, piece), ("rep", "section"), 0, 0, tiled=True
    ).reshape(replica_total, section_total, slots, rows, piece)

    slopes = jnp.stack([slope_first, slope_second]).reshape(slots, 2, tokens, width)
    slopes_own = lax.dynamic_index_in_dim(slopes, core, 1, keepdims=False)
    slopes_sib = lax.ppermute(lax.dynamic_index_in_dim(slopes, 1 - core, 1, keepdims=False), "section", swap)
    slope_all = jnp.concatenate([slopes_own, slopes_sib])

    g = by_cut(lax.dynamic_index_in_dim(top_grad[0], core, 0, keepdims=False))
    down = [(i, i - 2) for i in range(2, section_total)]
    g_at, head_at = [None] * layers, [None] * layers
    for layer in reversed(range(layers)):
        own = (my_map[layer] % 2 == core).astype(jnp.int32)
        pick = jnp.stack([own, my_slot[layer]])
        slope_spec = pl.BlockSpec((1, tokens, width), lambda i, p: ((1 - p[0]) * slots + p[1], 0, 0))
        g_at[layer] = g
        head_shape = jax.ShapeDtypeStruct((tokens, width), BF16)
        if layer == 0:
            (head_at[layer],) = call(
                last_layer_kernel,
                pick,
                (g, slope_all, o_own, o_sib),
                [whole(g), slope_spec, ANY, ANY],
                (head_shape,),
                weight_shape,
                1,
            )
            break
        parts, head_at[layer] = call(
            backward_kernel,
            pick,
            (g, slope_all, o_own, o_sib, v_own, v_sib),
            [whole(g), slope_spec, ANY, ANY, ANY, ANY],
            (jax.ShapeDtypeStruct(g.shape, BF16), head_shape),
            weight_shape,
            2,
        )
        mine = reduce_slices(parts, g)
        distance = chip_of[:, layer] - chip_of[:, layer - 1]
        my_distance = lax.dynamic_index_in_dim(distance, rep, 0, keepdims=False)

        def hop(i, value, my_distance=my_distance):
            came = lax.ppermute(value, "section", down)
            return jnp.where(i < my_distance, came, value)

        mine = lax.fori_loop(0, jnp.max(distance), hop, mine)
        g = gather_slices(mine)

    g_window = lax.dynamic_slice_in_dim(jnp.stack(g_at), my_window, window, 0)
    head_window = lax.dynamic_slice_in_dim(jnp.stack(head_at), my_window, window, 0)
    g_send = g_window.reshape(window, tp_total, tokens, 2, piece).transpose(1, 3, 0, 2, 4)
    g_all = lax.all_to_all(g_send.reshape(owners, window, tokens, piece), ("rep", "section"), 0, 0, tiled=True)
    head_send = jnp.broadcast_to(head_window[None], (owners,) + head_window.shape)
    head_all = lax.all_to_all(head_send, ("rep", "section"), 0, 0, tiled=True)
    by_chip = (replica_total, section_total // 2, 2, window, tokens)
    return gradients(
        section_map,
        position,
        slot_of,
        x_all,
        head_all.reshape(by_chip + (width,)),
        g_all.reshape(by_chip + (piece,)),
        act_all,
    )


def solution(mesh):
    placed = (
        P(),
        P("rep", "section", None, None, None),
        P("rep", None, None, None),
        P("rep", "section", None, "tp"),
        P("rep", "section", None, "tp"),
    )
    return jax.shard_map(
        per_device,
        mesh=mesh,
        in_specs=placed,
        out_specs=(P(None, ("rep", "section"), "tp"), P(None, ("rep", "section"), "tp")),
        check_vma=False,
    )
```

time: 2070 us -> 517 us (0.25)
  waiting for transfers between devices: 1650 us -> 207 us
  matrix products: 166 us -> 0 us
  Pallas kernels: 0 us -> 72.1 us
  other arithmetic: 79.4 us -> 30.9 us
  starting transfers between devices: 77.7 us -> 110 us
  local copies, waits for them, and re-layouts: 76.4 us -> 51.1 us
    psum x19 -> x0, waiting for transfers between devices: 1350 us -> none  [add_heads(): summed = lax.psum(term.astype(jnp.bfloat16), 'tp').astype(jnp.float32)]
    dot_general x44 -> x0, matrix products: 166 us -> none  [the longest x18 75.3 us: one_turn(): jnp.dot(upstream, out_weight[0, slot_index], preferred_element_type=jnp.f...]
    all_to_all x1 -> x19, starting transfers between devices: 6.33 us -> 101 us  [the longest x8 34.1 us: reduce_slices(): got = lax.all_to_all(parts, 'tp', 0, 0, tiled=True)]
    pallas_call x0 -> x11, Pallas kernels: none -> 72.1 us  [the longest x10 63.8 us: call(): pl.pallas_call(functools.partial(kernel, chunks), out_shape=outs, grid_sp...]
    ppermute x9 -> x7, starting transfers between devices: 70.9 us -> 8.67 us  [the longest x4 5.17 us: hop(): came = lax.ppermute(value, 'section', down)]
    ppermute x9 -> x7, waiting for transfers between devices: 73.2 us -> 12.3 us  [the longest x4 12.3 us: hop(): came = lax.ppermute(value, 'section', down)]
    scatter x18 -> x0, other arithmetic: 46.9 us -> none  [one_turn(): grad_store.at[slot_index, micro_index]]
    all_to_all x1 -> x19, waiting for transfers between devices: 224 us -> 192 us  [the longest x8 53.2 us: reduce_slices(): got = lax.all_to_all(parts, 'tp', 0, 0, tiled=True)]
  transfers between devices with their start and end apart: 29 -> 27, of which waited for: 29 -> 23; matrix products, arithmetic and copies ran while one was open for 1% -> 10% of each run, Pallas kernels for 0% -> 3%
where the time goes in v1:
time: 517 us; the launch traced here: 513 us
  waiting for transfers between devices  207 us (40%)
  starting transfers between devices  110 us (21%)
  Pallas kernels  72.1 us (14%)
  local copies, waits for them, and re-layouts  51.1 us (10%)
  between operations  32.3 us (6%)
  other arithmetic  30.9 us (6%)
  loops' own time  9.4 us (2%)
    pallas_call x10, Pallas kernels, call(): pl.pallas_call(functools.partial(kernel, chunks), out_shape=outs, grid_sp...  63.8 us
    all_to_all x8, waiting for transfers between devices, reduce_slices(): got = lax.all_to_all(parts, 'tp', 0, 0, tiled=True)  53.2 us
    all_to_all x1, waiting for transfers between devices, per_device(): head_all = lax.all_to_all(head_send, ('rep', 'section'), 0, 0, tiled=True)  52.8 us
    all_to_all x8, waiting for transfers between devices, gather_slices(): return lax.all_to_all(spread, 'tp', 0, 0, tiled=True)  41.9 us
    all_to_all x8, starting transfers between devices, reduce_slices(): got = lax.all_to_all(parts, 'tp', 0, 0, tiled=True)  34.1 us
    all_to_all x8, starting transfers between devices, gather_slices(): return lax.all_to_all(spread, 'tp', 0, 0, tiled=True)  32.8 us
    all_to_all x1, waiting for transfers between devices, per_device(): lax.all_to_all(g_send.reshape(owners, window, tokens, piece), ('rep', 'se...  28.9 us
    all_to_all x1, starting transfers between devices, per_device(): lax.all_to_all(xs.transpose(1, 3, 0, 2, 4).reshape(owners, slots, rows, p...  25 us
  transfers between devices with their start and end apart: 27, of which 23 were waited for; matrix products, arithmetic and copies ran while one was open for 10% of the time, Pallas kernels for 3%

profile of v1, /device:TPU:1, one launch (start us, length us, event | category | flops | bytes accessed | tf_op | source)
XLA Modules:
  0.0 513.1 jit_solution(2226717584284286902)
XLA Ops:
  11.4 7.7 %shard_map.86 = (bf16[8,128,512]{2,1,0:T(8,128)(2,1)}, bf16[128,512]{1,0:T(8,128)(2,1)S(1)}, f32[128,512]{1,0:T(8,128)S(1)}) custom-call(s32[2]{0:T(128)S(1)} %copy-done.23, bf16[8,128,512]{2,1,0:T(8,128)(2,1)S(1)} %bitcast.141, bf16[2,4096,512]{2,1,0:T(8,128)(2,1)} %bitcast.149, bf16[2,4096,512]{2,1,0:T(8,128)(2,1)} %bitcast.159), custom_call_target="tpu_custom_call" | custom-call | flops 1073741824 | bytes 8388608 | tf_op jit(solution)/shard_map/pallas_call | solution.py:100
  26.8 13.5 %all-to-all-done = bf16[8,128,512]{2,1,0:T(8,128)(2,1)S(1)} async-done(((bf16[8,128,512]{2,1,0:T(8,128)(2,1)}), bf16[8,128,512]{2,1,0:T(8,128)(2,1)S(1)}, u32[]{:S(2)}, u32[]{:S(2)}) %all-to-all-start) | async-done | bytes 1048608 | tf_op jit(solution)/shard_map/all_to_all | solution.py:203
  47.2 13.4 %all-to-all-done.1.x_ref = bf16[8,128,512]{2,1,0:T(8,128)(2,1)S(1)} async-done(((bf16[8,128,512]{2,1,0:T(8,128)(2,1)}), bf16[8,128,512]{2,1,0:T(8,128)(2,1)S(1)}, u32[]{:S(2)}, u32[]{:S(2)}) %all-to-all-start.1) | async-done | bytes 1048608 | tf_op jit(solution)/shard_map/all_to_all | solution.py:209
  73.5 6.4 %shard_map.88 = (bf16[8,64,512]{2,1,0:T(8,128)(2,1)S(1)}, bf16[64,512]{1,0:T(8,128)(2,1)S(1)}) custom-call(s32[2]{0:T(128)S(1)} %pad_add_fusion.2.pick_ref, bf16[8,64,512]{2,1,0:T(8,128)(2,1)S(1)} %bitcast.143, f32[4,64,512]{2,1,0:T(8,128)S(1)} %pad_maximum_fusion.slope_ref, bf16[2,4096,512]{2,1,0:T(8,128)(2,1)} %bitcast.160, ...), custom_call_target="tpu_custom_call" | custom-call | flops 536870912 | bytes 8388608 | tf_op jit(solution)/shard_map/pallas_call | solution.py:100
  101.7 6.3 %all-to-all-done.4.g_ref = bf16[8,64,512]{2,1,0:T(8,128)(2,1)S(1)} async-done(((bf16[8,64,512]{2,1,0:T(8,128)(2,1)}), bf16[8,64,512]{2,1,0:T(8,128)(2,1)S(1)}, u32[]{:S(2)}, u32[]{:S(2)}) %all-to-all-start.4) | async-done | bytes 524320 | tf_op jit(solution)/shard_map/all_to_all | solution.py:209
  108.0 6.4 %shard_map.89 = (bf16[8,64,512]{2,1,0:T(8,128)(2,1)S(1)}, bf16[64,512]{1,0:T(8,128)(2,1)S(1)}) custom-call(s32[2]{0:T(128)S(1)} %pad_add_fusion.3.pick_ref, bf16[8,64,512]{2,1,0:T(8,128)(2,1)S(1)} %all-to-all-done.4.g_ref, f32[4,64,512]{2,1,0:T(8,128)S(1)} %pad_maximum_fusion.slope_ref, bf16[2,4096,512]{2,1,0:T(8,128)(2,1)} %bitcast.161, ...), custom_call_target="tpu_custom_call" | custom-call | flops 536870912 | bytes 8388608 | tf_op jit(solution)/shard_map/pallas_call | solution.py:100
  120.0 7.6 %all-to-all-done.5 = bf16[8,64,512]{2,1,0:T(8,128)(2,1)} async-done(((bf16[8,64,512]{2,1,0:T(8,128)(2,1)}), bf16[8,64,512]{2,1,0:T(8,128)(2,1)}, u32[]{:S(2)}, u32[]{:S(2)}) %all-to-all-start.5) | async-done | bytes 524320 | tf_op jit(solution)/shard_map/all_to_all | solution.py:203
  147.1 7.4 %shard_map.90 = (bf16[8,64,512]{2,1,0:T(8,128)(2,1)S(1)}, bf16[64,512]{1,0:T(8,128)(2,1)S(1)}) custom-call(s32[2]{0:T(128)S(1)} %pad_add_fusion.4.pick_ref, bf16[8,64,512]{2,1,0:T(8,128)(2,1)} %all-to-all-done.6.g_ref, f32[4,64,512]{2,1,0:T(8,128)S(1)} %pad_maximum_fusion.slope_ref, bf16[2,4096,512]{2,1,0:T(8,128)(2,1)} %bitcast.162, ...), custom_call_target="tpu_custom_call" | custom-call | flops 536870912 | bytes 8388608 | tf_op jit(solution)/shard_map/pallas_call | solution.py:100
  160.7 6.4 %all-to-all-done.7 = bf16[8,64,512]{2,1,0:T(8,128)(2,1)} async-done(((bf16[8,64,512]{2,1,0:T(8,128)(2,1)}), bf16[8,64,512]{2,1,0:T(8,128)(2,1)}, u32[]{:S(2)}, u32[]{:S(2)}) %all-to-all-start.7) | async-done | bytes 524320 | tf_op jit(solution)/shard_map/all_to_all | solution.py:203
  182.0 7.4 %shard_map.91 = (bf16[8,64,512]{2,1,0:T(8,128)(2,1)S(1)}, bf16[64,512]{1,0:T(8,128)(2,1)S(1)}) custom-call(s32[2]{0:T(128)S(1)} %pad_add_fusion.5.pick_ref, bf16[8,64,512]{2,1,0:T(8,128)(2,1)} %all-to-all-done.8.g_ref, f32[4,64,512]{2,1,0:T(8,128)S(1)} %pad_maximum_fusion.slope_ref, bf16[2,4096,512]{2,1,0:T(8,128)(2,1)} %bitcast.163, ...), custom_call_target="tpu_custom_call" | custom-call | flops 536870912 | bytes 8388608 | tf_op jit(solution)/shard_map/pallas_call | solution.py:100
  195.5 6.5 %all-to-all-done.9 = bf16[8,64,512]{2,1,0:T(8,128)(2,1)} async-done(((bf16[8,64,512]{2,1,0:T(8,128)(2,1)}), bf16[8,64,512]{2,1,0:T(8,128)(2,1)}, u32[]{:S(2)}, u32[]{:S(2)}) %all-to-all-start.9) | async-done | bytes 524320 | tf_op jit(solution)/shard_map/all_to_all | solution.py:203
  204.0 6.3 %while.73 = (s32[]{:T(128)}, bf16[64,512]{1,0:T(8,128)(2,1)S(1)}, s32[]{:T(128)}, s32[]{:T(128)}, s32[]{:T(128)}) while((s32[]{:T(128)}, bf16[64,512]{1,0:T(8,128)(2,1)S(1)}, s32[]{:T(128)}, s32[]{:T(128)}, s32[]{:T(128)}) %tuple.143), condition=%wide.region_18.19_spmd, body=%wide.region_17.18_spmd.sunk | while | flops 32771 | bytes 458863 | solution.py:283
  222.3 7.4 %shard_map.92 = (bf16[8,64,512]{2,1,0:T(8,128)(2,1)S(1)}, bf16[64,512]{1,0:T(8,128)(2,1)S(1)}) custom-call(s32[2]{0:T(128)S(1)} %pad_add_fusion.6.pick_ref, bf16[8,64,512]{2,1,0:T(8,128)(2,1)} %all-to-all-done.10.g_ref, f32[4,64,512]{2,1,0:T(8,128)S(1)} %pad_maximum_fusion.slope_ref, bf16[2,4096,512]{2,1,0:T(8,128)(2,1)} %bitcast.164, ...), custom_call_target="tpu_custom_call" | custom-call | flops 536870912 | bytes 8388608 | tf_op jit(solution)/shard_map/pallas_call | solution.py:100
  235.8 6.5 %all-to-all-done.11 = bf16[8,64,512]{2,1,0:T(8,128)(2,1)} async-done(((bf16[8,64,512]{2,1,0:T(8,128)(2,1)}), bf16[8,64,512]{2,1,0:T(8,128)(2,1)}, u32[]{:S(2)}, u32[]{:S(2)}) %all-to-all-start.11) | async-done | bytes 524320 | tf_op jit(solution)/shard_map/all_to_all | solution.py:203
  256.9 7.4 %shard_map.93 = (bf16[8,64,512]{2,1,0:T(8,128)(2,1)S(1)}, bf16[64,512]{1,0:T(8,128)(2,1)S(1)}) custom-call(s32[2]{0:T(128)S(1)} %pad_add_fusion.7.pick_ref, bf16[8,64,512]{2,1,0:T(8,128)(2,1)} %all-to-all-done.12.g_ref, f32[4,64,512]{2,1,0:T(8,128)S(1)} %pad_maximum_fusion.slope_ref, bf16[2,4096,512]{2,1,0:T(8,128)(2,1)} %bitcast.165, ...), custom_call_target="tpu_custom_call" | custom-call | flops 536870912 | bytes 8388608 | tf_op jit(solution)/shard_map/pallas_call | solution.py:100
  270.4 6.5 %all-to-all-done.13 = bf16[8,64,512]{2,1,0:T(8,128)(2,1)} async-done(((bf16[8,64,512]{2,1,0:T(8,128)(2,1)}), bf16[8,64,512]{2,1,0:T(8,128)(2,1)}, u32[]{:S(2)}, u32[]{:S(2)}) %all-to-all-start.13) | async-done | bytes 524320 | tf_op jit(solution)/shard_map/all_to_all | solution.py:203
  278.9 6.3 %while.75 = (s32[]{:T(128)}, bf16[64,512]{1,0:T(8,128)(2,1)S(1)}, s32[]{:T(128)}, s32[]{:T(128)}, s32[]{:T(128)}) while((s32[]{:T(128)}, bf16[64,512]{1,0:T(8,128)(2,1)S(1)}, s32[]{:T(128)}, s32[]{:T(128)}, s32[]{:T(128)}) %tuple.149), condition=%wide.region_26.27_spmd, body=%wide.region_25.26_spmd.sunk | while | flops 32771 | bytes 458863 | solution.py:283
  297.2 7.4 %shard_map.94 = (bf16[8,64,512]{2,1,0:T(8,128)(2,1)S(1)}, bf16[64,512]{1,0:T(8,128)(2,1)S(1)}) custom-call(s32[2]{0:T(128)S(1)} %pad_add_fusion.8.pick_ref, bf16[8,64,512]{2,1,0:T(8,128)(2,1)} %all-to-all-done.14.g_ref, f32[4,64,512]{2,1,0:T(8,128)S(1)} %pad_maximum_fusion.slope_ref, bf16[2,4096,512]{2,1,0:T(8,128)(2,1)} %bitcast.166, ...), custom_call_target="tpu_custom_call" | custom-call | flops 536870912 | bytes 8388608 | tf_op jit(solution)/shard_map/pallas_call | solution.py:100
  319.4 6.4 %while.76 = (s32[]{:T(128)}, bf16[64,512]{1,0:T(8,128)(2,1)S(1)}, s32[]{:T(128)}, s32[]{:T(128)}, s32[]{:T(128)}) while((s32[]{:T(128)}, bf16[64,512]{1,0:T(8,128)(2,1)S(1)}, s32[]{:T(128)}, s32[]{:T(128)}, s32[]{:T(128)}) %tuple.152), condition=%wide.region_30.31_spmd, body=%wide.region_29.30_spmd.sunk | while | flops 32771 | bytes 458863 | solution.py:283
  340.8 25.0 %all-to-all-start.2 = ((bf16[16,2,128,256]{3,2,1,0:T(8,128)(2,1)}), bf16[16,2,128,256]{3,2,1,0:T(8,128)(2,1)S(1)}, u32[]{:S(2)}, u32[]{:S(2)}) async-start(bf16[16,2,128,256]{3,2,1,0:T(8,128)(2,1)} %bitcast.171), calls=%async_computation.2 | async-start | bytes 4194304 | tf_op jit(solution)/shard_map/all_to_all | solution.py:237
  381.5 15.6 %all-to-all-done.2 = bf16[16,2,128,256]{3,2,1,0:T(8,128)(2,1)S(1)} async-done(((bf16[16,2,128,256]{3,2,1,0:T(8,128)(2,1)}), bf16[16,2,128,256]{3,2,1,0:T(8,128)(2,1)S(1)}, u32[]{:S(2)}, u32[]{:S(2)}) %all-to-all-start.2) | async-done | bytes 2097184 | tf_op jit(solution)/shard_map/all_to_all | solution.py:237
  406.0 28.9 %all-to-all-done.18 = bf16[16,4,64,256]{3,2,1,0:T(8,128)(2,1)} async-done(((bf16[16,4,64,256]{3,2,1,0:T(8,128)(2,1)}), bf16[16,4,64,256]{3,2,1,0:T(8,128)(2,1)}, u32[]{:S(2)}, u32[]{:S(2)}) %all-to-all-start.18) | async-done | bytes 2097184 | tf_op jit(solution)/shard_map/all_to_all | solution.py:289
  445.0 52.8 %all-to-all-done.17 = bf16[16,4,64,512]{3,2,1,0:T(8,128)(2,1)} async-done(((bf16[16,4,64,512]{3,2,1,0:T(8,128)(2,1)}), bf16[16,4,64,512]{3,2,1,0:T(8,128)(2,1)}, u32[]{:S(2)}, u32[]{:S(2)}) %all-to-all-start.17) | async-done | bytes 4194336 | tf_op jit(solution)/shard_map/all_to_all | solution.py:291
  497.9 8.3 %shard_map.96 = (bf16[8,256,512]{2,1,0:T(8,128)(2,1)}, bf16[8,256,512]{2,1,0:T(8,128)(2,1)}) custom-call(s32[3,2,8]{2,1,0:T(2,128)S(1)} %pad_add_fusion.tab_ref, bf16[2,8,2,128,256]{4,3,2,1,0:T(8,128)(2,1)S(1)} %bitcast.139, bf16[2,8,2,128,256]{4,3,2,1,0:T(8,128)(2,1)S(1)} %bitcast.140, bf16[2,4,2,4,64,512]{5,4,3,2,1,0:T(8,128)(2,1)} %bitcast.63.h0.h1, ...), custom_call_target="tpu_custom_call" | custom-call | tf_op jit(solution)/shard_map/pallas_call | solution.py:153
  (214 shorter events, 224.3 us)
Async XLA Ops:
  7.2 66.3 %collective-permute-start.8 = (bf16[2,4096,512]{2,1,0:T(8,128)(2,1)}, bf16[2,4096,512]{2,1,0:T(8,128)(2,1)}, u32[]{:S(2)}, u32[]{:S(2)}) collective-permute-start(bf16[2,4096,512]{2,1,0:T(8,128)(2,1)} %bitcast.158), channel_id=1, source_target_pairs={{0,8},{8,0},{16,24},{24,16},{32,40},{40,32},{48,56},{56,48},{1,9},... | collective-permute-start | bytes 25165832 | tf_op jit(solution)/shard_map/ppermute | solution.py:196
  8.7 64.8 %collective-permute-start.9 = (bf16[2,4096,512]{2,1,0:T(8,128)(2,1)}, bf16[2,4096,512]{2,1,0:T(8,128)(2,1)}, u32[]{:S(2)}, u32[]{:S(2)}) collective-permute-start(bf16[2,4096,512]{2,1,0:T(8,128)(2,1)} %bitcast.148), channel_id=1, source_target_pairs={{0,8},{8,0},{16,24},{24,16},{32,40},{40,32},{48,56},{56,48},{1,9},... | collective-permute-start | bytes 25165832 | tf_op jit(solution)/shard_map/ppermute | solution.py:197
  19.1 21.3 %all-to-all-start = ((bf16[8,128,512]{2,1,0:T(8,128)(2,1)}), bf16[8,128,512]{2,1,0:T(8,128)(2,1)S(1)}, u32[]{:S(2)}, u32[]{:S(2)}) async-start(bf16[8,128,512]{2,1,0:T(8,128)(2,1)} %get-tuple-element.182), calls=%async_computation | async-start | bytes 2097152 | tf_op jit(solution)/shard_map/all_to_all | solution.py:203
  42.5 18.1 %all-to-all-start.1 = ((bf16[8,128,512]{2,1,0:T(8,128)(2,1)}), bf16[8,128,512]{2,1,0:T(8,128)(2,1)S(1)}, u32[]{:S(2)}, u32[]{:S(2)}) async-start(bf16[8,128,512]{2,1,0:T(8,128)(2,1)} %broadcast_in_dim.18), calls=%async_computation.1 | async-start | bytes 2097152 | tf_op jit(solution)/shard_map/all_to_all | solution.py:209
  64.6 7.2 %collective-permute-start.7 = (f32[2,64,512]{2,1,0:T(8,128)}, f32[2,64,512]{2,1,0:T(8,128)S(1)}, u32[]{:S(2)}, u32[]{:S(2)}) collective-permute-start(f32[2,64,512]{2,1,0:T(8,128)} %get-tuple-element.281), channel_id=1, source_target_pairs={{0,8},{8,0},{16,24},{24,16},{32,40},{40,32},{48,56},{56,48},{1,9},... | collective-permute-start | bytes 786440 | tf_op jit(solution)/shard_map/ppermute | solution.py:243
  80.8 13.1 %all-to-all-start.3 = ((bf16[8,64,512]{2,1,0:T(8,128)(2,1)}), bf16[8,64,512]{2,1,0:T(8,128)(2,1)S(1)}, u32[]{:S(2)}, u32[]{:S(2)}) async-start(bf16[8,64,512]{2,1,0:T(8,128)(2,1)} %copy-done.5), calls=%async_computation.3 | async-start | bytes 1048576 | tf_op jit(solution)/shard_map/all_to_all | solution.py:203
  95.5 12.5 %all-to-all-start.4 = ((bf16[8,64,512]{2,1,0:T(8,128)(2,1)}), bf16[8,64,512]{2,1,0:T(8,128)(2,1)S(1)}, u32[]{:S(2)}, u32[]{:S(2)}) async-start(bf16[8,64,512]{2,1,0:T(8,128)(2,1)} %broadcast_in_dim.19), calls=%async_computation.4 | async-start | bytes 1048576 | tf_op jit(solution)/shard_map/all_to_all | solution.py:209
  115.2 12.3 %all-to-all-start.5 = ((bf16[8,64,512]{2,1,0:T(8,128)(2,1)}), bf16[8,64,512]{2,1,0:T(8,128)(2,1)}, u32[]{:S(2)}, u32[]{:S(2)}) async-start(bf16[8,64,512]{2,1,0:T(8,128)(2,1)} %copy-done.6), calls=%async_computation.5 | async-start | bytes 1048576 | tf_op jit(solution)/shard_map/all_to_all | solution.py:203
  129.3 5.0 collective-permute-start.1
  135.7 11.4 %all-to-all-start.6 = ((bf16[8,64,512]{2,1,0:T(8,128)(2,1)}), bf16[8,64,512]{2,1,0:T(8,128)(2,1)}, u32[]{:S(2)}, u32[]{:S(2)}) async-start(bf16[8,64,512]{2,1,0:T(8,128)(2,1)} %broadcast_in_dim.20), calls=%async_computation.6 | async-start | bytes 1048576 | tf_op jit(solution)/shard_map/all_to_all | solution.py:209
  156.0 11.2 %all-to-all-start.7 = ((bf16[8,64,512]{2,1,0:T(8,128)(2,1)}), bf16[8,64,512]{2,1,0:T(8,128)(2,1)}, u32[]{:S(2)}, u32[]{:S(2)}) async-start(bf16[8,64,512]{2,1,0:T(8,128)(2,1)} %copy-done.7), calls=%async_computation.7 | async-start | bytes 1048576 | tf_op jit(solution)/shard_map/all_to_all | solution.py:203
  170.6 11.3 %all-to-all-start.8 = ((bf16[8,64,512]{2,1,0:T(8,128)(2,1)}), bf16[8,64,512]{2,1,0:T(8,128)(2,1)}, u32[]{:S(2)}, u32[]{:S(2)}) async-start(bf16[8,64,512]{2,1,0:T(8,128)(2,1)} %broadcast_in_dim.21), calls=%async_computation.8 | async-start | bytes 1048576 | tf_op jit(solution)/shard_map/all_to_all | solution.py:209
  190.8 11.2 %all-to-all-start.9 = ((bf16[8,64,512]{2,1,0:T(8,128)(2,1)}), bf16[8,64,512]{2,1,0:T(8,128)(2,1)}, u32[]{:S(2)}, u32[]{:S(2)}) async-start(bf16[8,64,512]{2,1,0:T(8,128)(2,1)} %copy-done.8), calls=%async_computation.9 | async-start | bytes 1048576 | tf_op jit(solution)/shard_map/all_to_all | solution.py:203
  211.1 11.2 %all-to-all-start.10 = ((bf16[8,64,512]{2,1,0:T(8,128)(2,1)}), bf16[8,64,512]{2,1,0:T(8,128)(2,1)}, u32[]{:S(2)}, u32[]{:S(2)}) async-start(bf16[8,64,512]{2,1,0:T(8,128)(2,1)} %broadcast_in_dim.22), calls=%async_computation.10 | async-start | bytes 1048576 | tf_op jit(solution)/shard_map/all_to_all | solution.py:209
  231.2 11.2 %all-to-all-start.11 = ((bf16[8,64,512]{2,1,0:T(8,128)(2,1)}), bf16[8,64,512]{2,1,0:T(8,128)(2,1)}, u32[]{:S(2)}, u32[]{:S(2)}) async-start(bf16[8,64,512]{2,1,0:T(8,128)(2,1)} %copy-done.9), calls=%async_computation.11 | async-start | bytes 1048576 | tf_op jit(solution)/shard_map/all_to_all | solution.py:203
  245.7 11.2 %all-to-all-start.12 = ((bf16[8,64,512]{2,1,0:T(8,128)(2,1)}), bf16[8,64,512]{2,1,0:T(8,128)(2,1)}, u32[]{:S(2)}, u32[]{:S(2)}) async-start(bf16[8,64,512]{2,1,0:T(8,128)(2,1)} %broadcast_in_dim.23), calls=%async_computation.12 | async-start | bytes 1048576 | tf_op jit(solution)/shard_map/all_to_all | solution.py:209
  265.8 11.2 %all-to-all-start.13 = ((bf16[8,64,512]{2,1,0:T(8,128)(2,1)}), bf16[8,64,512]{2,1,0:T(8,128)(2,1)}, u32[]{:S(2)}, u32[]{:S(2)}) async-start(bf16[8,64,512]{2,1,0:T(8,128)(2,1)} %copy-done.10), calls=%async_computation.13 | async-start | bytes 1048576 | tf_op jit(solution)/shard_map/all_to_all | solution.py:203
  286.1 11.2 %all-to-all-start.14 = ((bf16[8,64,512]{2,1,0:T(8,128)(2,1)}), bf16[8,64,512]{2,1,0:T(8,128)(2,1)}, u32[]{:S(2)}, u32[]{:S(2)}) async-start(bf16[8,64,512]{2,1,0:T(8,128)(2,1)} %broadcast_in_dim.24), calls=%async_computation.14 | async-start | bytes 1048576 | tf_op jit(solution)/shard_map/all_to_all | solution.py:209
  306.1 11.3 %all-to-all-start.15 = ((bf16[8,64,512]{2,1,0:T(8,128)(2,1)}), bf16[8,64,512]{2,1,0:T(8,128)(2,1)}, u32[]{:S(2)}, u32[]{:S(2)}) async-start(bf16[8,64,512]{2,1,0:T(8,128)(2,1)} %copy-done.4), calls=%async_computation.15 | async-start | bytes 1048576 | tf_op jit(solution)/shard_map/all_to_all | solution.py:203
  326.6 13.3 %all-to-all-start.16 = ((bf16[8,64,512]{2,1,0:T(8,128)(2,1)}), bf16[8,64,512]{2,1,0:T(8,128)(2,1)S(1)}, u32[]{:S(2)}, u32[]{:S(2)}) async-start(bf16[8,64,512]{2,1,0:T(8,128)(2,1)} %broadcast_in_dim.25), calls=%async_computation.16 | async-start | bytes 1048576 | tf_op jit(solution)/shard_map/all_to_all | solution.py:209
  331.4 113.6 %all-gather.3.cloned.1.call-start = ((), (), s32[]{:S(2)}) async-start(), calls=%async_computation.19 | async-start | bytes 4456448 | tf_op jit(solution)/shard_map/all_gather | solution.py:234
  340.8 56.4 %all-to-all-start.2 = ((bf16[16,2,128,256]{3,2,1,0:T(8,128)(2,1)}), bf16[16,2,128,256]{3,2,1,0:T(8,128)(2,1)S(1)}, u32[]{:S(2)}, u32[]{:S(2)}) async-start(bf16[16,2,128,256]{3,2,1,0:T(8,128)(2,1)} %bitcast.171), calls=%async_computation.2 | async-start | bytes 4194304 | tf_op jit(solution)/shard_map/all_to_all | solution.py:237
  397.1 37.8 %all-to-all-start.18 = ((bf16[16,4,64,256]{3,2,1,0:T(8,128)(2,1)}), bf16[16,4,64,256]{3,2,1,0:T(8,128)(2,1)}, u32[]{:S(2)}, u32[]{:S(2)}) async-start(bf16[16,4,64,256]{3,2,1,0:T(8,128)(2,1)} %bitcast.170), calls=%async_computation.18 | async-start | bytes 4194304 | tf_op jit(solution)/shard_map/all_to_all | solution.py:289
  437.4 60.4 %all-to-all-start.17 = ((bf16[16,4,64,512]{3,2,1,0:T(8,128)(2,1)}), bf16[16,4,64,512]{3,2,1,0:T(8,128)(2,1)}, u32[]{:S(2)}, u32[]{:S(2)}) async-start(bf16[16,4,64,512]{3,2,1,0:T(8,128)(2,1)} %broadcast_in_dim.26), calls=%async_computation.17 | async-start | bytes 8388608 | tf_op jit(solution)/shard_map/all_to_all | solution.py:291
  (38 other events, 269.4 us)
Sparse Core Ops, SparseCore 0:
  334.7 110.3 all-gather.2

commit v2 on v0

v2 whole, which is shorter than its diff:
```python
import functools

import jax
import jax.numpy as jnp
from jax import lax
from jax.experimental import pallas as pl
from jax.experimental.pallas import tpu as pltpu
from jax.sharding import PartitionSpec as P

BF16 = jnp.bfloat16
F32 = jnp.float32
VMEM_BYTES = 48 * 1024 * 1024
NT = (((1,), (1,)), ((), ()))
TN = (((0,), (0,)), ((), ()))
ANY = pl.BlockSpec(memory_space=pl.ANY)
HBM = pl.BlockSpec(memory_space=pltpu.HBM)
SMEM = pl.BlockSpec(memory_space=pltpu.SMEM)
VMEM = pl.BlockSpec(memory_space=pltpu.VMEM)


def silu_slope(preact):
    sigma = jax.nn.sigmoid(preact)
    return sigma * (1.0 + preact * (1.0 - sigma))


def run(kernel, operands, specs, outs, out_specs, scratch, bytes_moved, flops=0):
    return pl.pallas_call(
        kernel,
        out_shape=outs,
        in_specs=specs,
        out_specs=out_specs,
        scratch_shapes=scratch,
        compiler_params=pltpu.CompilerParams(vmem_limit_bytes=VMEM_BYTES),
        cost_estimate=pl.CostEstimate(flops=flops, bytes_accessed=bytes_moved, transcendentals=0),
    )(*operands)


class Feed:
    def __init__(self, sources, buffer, sems, chunks):
        self.last = sources[-1][1]
        self.buffer, self.sems = buffer, sems
        for condition, place in sources:

            def begin(place=place):
                for i in range(chunks):
                    pltpu.make_async_copy(place(i), buffer.at[i], sems.at[i]).start()

            if condition is None:
                begin()
            else:
                pl.when(condition)(begin)

    def take(self, i):
        pltpu.make_async_copy(self.last(i), self.buffer.at[i], self.sems.at[i]).wait()
        return self.buffer[i]


def weight_places(scalars, refs, cut):
    slot = scalars[1]

    def place(ref):
        return lambda i: ref.at[slot, pl.ds(i * cut, cut)]

    if len(refs) == 1:
        return [(None, place(refs[0]))]
    return [(scalars[0] == 1, place(refs[0])), (scalars[0] == 0, place(refs[1]))]


def rows_place(ref, core, cut):
    if ref.shape[-1] == cut:
        return lambda i: ref.at[i]
    if len(ref.shape) == 2:
        return lambda i: ref.at[:, pl.ds(i * cut, cut)]
    return lambda i: ref.at[core, :, pl.ds(i * cut, cut)]


def dot_in(rows, weight, chunks):
    total = None
    for i in range(chunks):
        part = jnp.dot(rows.take(i), weight.take(i), preferred_element_type=F32)
        total = part if total is None else total + part
    return total


def dot_out(rows, weight, chunks, stage, part_ref, sems):
    copies = []
    for i in range(chunks):
        stage[i] = lax.dot_general(rows, weight.take(i), NT, preferred_element_type=F32).astype(BF16)
        copies.append(pltpu.make_async_copy(stage.at[i], part_ref.at[i], sems.at[i]))
        copies[-1].start()
    return copies


def recompute(chunks, with_parts, scalars, x_ref, v_ref, *refs):
    o_ref, refs = (refs[0], refs[1:]) if with_parts else (None, refs)
    part_ref, refs = (refs[0], refs[1:]) if with_parts else (None, refs)
    act_mine, act_other, slope_mine, slope_other, xbuf, vbuf, act_rows, slope_rows, xsem, vsem = refs[:10]
    cut = vbuf.shape[1]
    core = scalars[2]
    x = Feed([(None, rows_place(x_ref, core, cut))], xbuf, xsem, chunks)
    v = Feed(weight_places(scalars, [v_ref], cut), vbuf, vsem, chunks)
    if with_parts:
        obuf, stage, osem, psem = refs[10:]
        o = Feed(weight_places(scalars, [o_ref], cut), obuf, osem, chunks)
    pre = dot_in(x, v, chunks)
    act = jax.nn.silu(pre).astype(BF16)
    copies = dot_out(act, o, chunks, stage, part_ref, psem) if with_parts else []
    act_rows[...] = act
    slope_rows[...] = silu_slope(pre)
    half = act_mine.shape[0]
    mine = pl.ds(pl.multiple_of(core * half, half), half)
    other = pl.ds(pl.multiple_of((1 - core) * half, half), half)
    act_mine[...] = act_rows[mine, :]
    act_other[...] = act_rows[other, :]
    slope_mine[...] = slope_rows[mine, :]
    slope_other[...] = slope_rows[other, :]
    for copy in copies:
        copy.wait()


def step(chunks, with_parts, deps, scalars, g_ref, *refs):
    slopes, refs = refs[:4], refs[4:]
    o_refs, refs = refs[:2], refs[2:]
    if with_parts:
        v_refs, refs = refs[:2], refs[2:]
    refs = refs[deps:]
    if with_parts:
        part_ref, refs = refs[0], refs[1:]
    head_ref, gbuf, sbuf, obuf, head_rows, gsem, ssem, osem, hsem = refs[:9]
    cut = obuf.shape[1]
    g = Feed([(None, rows_place(g_ref, scalars[2], cut))], gbuf, gsem, chunks)
    o = Feed(weight_places(scalars, o_refs, cut), obuf, osem, chunks)
    which = (1 - scalars[0]) * 2 + scalars[1]
    slope = Feed([(which == j, lambda i, ref=slopes[j]: ref) for j in range(4)], sbuf, ssem, 1)
    if with_parts:
        vbuf, stage, vsem, psem = refs[9:]
        v = Feed(weight_places(scalars, v_refs, cut), vbuf, vsem, chunks)
    act_grad = dot_in(g, o, chunks)
    head = (act_grad * slope.take(0)).astype(BF16)
    head_rows[...] = head
    out = pltpu.make_async_copy(head_rows, head_ref, hsem.at[0])
    out.start()
    copies = dot_out(head, v, chunks, stage, part_ref, psem) if with_parts else []
    for copy in copies + [out]:
        copy.wait()


def reduce_kernel(scalars, got_ref, base_ref, mine_ref, base, sem):
    cut = base.shape[1]
    place = rows_place(base_ref, scalars[2], cut)(scalars[3])
    copy = pltpu.make_async_copy(place, base, sem.at[0])
    copy.start()
    total = got_ref[0].astype(F32)
    for i in range(1, got_ref.shape[0]):
        total += got_ref[i].astype(F32)
    copy.wait()
    mine_ref[...] = (base[...].astype(F32) + total).astype(BF16)


def carve_kernel(count, scalars, *refs):
    heads, grads, outs, sems = refs[:count], refs[count : 2 * count], refs[2 * count : -1], refs[-1]
    chip, core = scalars[0], scalars[1]
    chips = len(outs)
    copies = []

    def copy(source, target):
        copies.append(pltpu.make_async_copy(source, target, sems.at[len(copies)]))
        copies[-1].start()

    for far, out in enumerate(outs):
        width = out.shape[-1] // 3
        to = lax.rem(chip + far, chips)
        for n in range(count):
            at = scalars[2 + n]
            copy(heads[n], out.at[at, :, pl.ds(0, width)])
            ref = grads[n]
            for replica in range(2):
                cut = replica * chips + to
                if ref.shape[-1] != width:
                    columns = pl.ds(pl.multiple_of(cut * width, width), width)
                    source = ref.at[:, columns] if len(ref.shape) == 2 else ref.at[core, :, columns]
                elif ref.shape[1] == out.shape[1]:
                    source = ref.at[cut]
                else:
                    source = ref.at[cut, pl.ds(pl.multiple_of(core * out.shape[1], out.shape[1]), out.shape[1])]
                copy(source, out.at[at, :, pl.ds((1 + replica) * width, width)])
    for one in copies:
        one.wait()


def pick_kernel(count, scalars, *refs):
    chips = 4
    sources, (own_out, own_here, sib_out, sib_here), sems = refs[:chips], refs[chips : chips + 4], refs[-1]
    core, rep = scalars[0], scalars[1]
    width = sources[0].shape[-1] // 3
    half = width // 2

    def columns(replica, side):
        return pl.ds(pl.multiple_of((1 + replica) * width + side * half, half), half)

    def moves(n, source, at):
        block = source.at[at]
        return [
            (block.at[:, pl.ds(0, width)], own_out.at[n, :, pl.ds(0, width)]),
            (block.at[:, columns(1 - rep, core)], own_out.at[n, :, pl.ds(width, half)]),
            (block.at[:, columns(rep, core)], own_here.at[n]),
            (block.at[:, pl.ds(0, width)], sib_out.at[n, :, pl.ds(0, width)]),
            (block.at[:, columns(1 - rep, 1 - core)], sib_out.at[n, :, pl.ds(width, half)]),
            (block.at[:, columns(rep, 1 - core)], sib_here.at[n]),
        ]

    for n in range(count):
        at = scalars[2 + 2 * n + 1]
        for far in range(chips):

            def begin(n=n, far=far, at=at):
                for k, (a, b) in enumerate(moves(n, sources[far], at)):
                    pltpu.make_async_copy(a, b, sems.at[n, k]).start()

            pl.when(scalars[2 + 2 * n] == far)(begin)
    for n in range(count):
        for k, (a, b) in enumerate(moves(n, sources[0], 0)):
            pltpu.make_async_copy(a, b, sems.at[n, k]).wait()


def gradient_kernel(first, *refs):
    (x0, xa1, x1, xa2, xa3, xa4), (g0, gh1, g1, gh2, gh3, gh4) = refs[:6], refs[6:12]
    value_ref, out_ref = refs[-2:]
    width = value_ref.shape[-1]

    def rows(alone0, with0, alone1, with1, with2, with3):
        narrow = [alone0[0], alone1[0], with2[0][:, width:], with3[0][:, width:]]
        wide = [with0[0][:, :width], with1[0][:, :width], with2[0][:, :width], with3[0][:, :width]]
        return jnp.concatenate(narrow, axis=0), jnp.concatenate(wide, axis=0)

    x, act = rows(x0, xa1, x1, xa2, xa3, xa4)
    g, head = rows(g0, gh1, g1, gh2, gh3, gh4)
    value_ref[0] = lax.dot_general(x, head, TN, preferred_element_type=F32).astype(BF16)
    out_ref[0] = lax.dot_general(g, act, TN, preferred_element_type=F32).astype(BF16)


def gradients(layers, first, count, forward, backward, before):
    piece = forward[0].shape[-1]
    width = forward[1].shape[-1] - piece
    out = jax.ShapeDtypeStruct((layers, piece, width), BF16)
    out_spec = pl.BlockSpec((1, piece, width), lambda l: (first + l, 0, 0))

    def block(array, start):
        return pl.BlockSpec((1,) + array.shape[1:], lambda l: (start + l, 0, 0))

    specs = [block(a, first) for a in forward] + [block(a, 0) for a in backward]
    operands = list(forward) + list(backward)
    aliases = {}
    if before is not None:
        aliases = {len(operands): 0, len(operands) + 1: 1}
        operands, specs = operands + list(before), specs + [ANY, ANY]
    return pl.pallas_call(
        functools.partial(gradient_kernel, first),
        out_shape=(out, out),
        grid=(count,),
        in_specs=specs,
        out_specs=(out_spec, out_spec),
        input_output_aliases=aliases,
        compiler_params=pltpu.CompilerParams(vmem_limit_bytes=VMEM_BYTES),
        cost_estimate=pl.CostEstimate(
            flops=count * 4 * piece * width * 256, bytes_accessed=count * 2400000, transcendentals=0
        ),
    )(*operands)


def per_device(section_map, checkpoint, top_grad, value_weight, out_weight):
    tp_total = lax.axis_size("tp")
    section_total = lax.axis_size("section")
    replica_total = lax.axis_size("rep")
    chips = section_total // 2
    rep, section, tp = (lax.axis_index(name) for name in ("rep", "section", "tp"))
    chip, core = section // 2, section % 2
    layers = section_map.shape[1]
    _, _, micro, tokens, model = checkpoint.shape
    slots, width = value_weight.shape[1], value_weight.shape[3]
    rows = micro * tokens
    cut = model // tp_total
    piece = model // (replica_total * section_total)
    v_own, o_own = value_weight[0], out_weight[0]
    x_pair, top_pair = checkpoint[0, 0], top_grad[0]

    first_of = jnp.sum(section_map[:, None, :] < section_map[:, :, None], axis=2).astype(jnp.int32)
    slot_of = jnp.arange(layers, dtype=jnp.int32)[None] - first_of
    my_map = lax.dynamic_index_in_dim(section_map, rep, 0, keepdims=False)
    my_slot = lax.dynamic_index_in_dim(slot_of, rep, 0, keepdims=False)
    my_chip = my_map // 2
    far_of = lax.rem(my_chip - chip + chips, chips)

    swap = [(i, i ^ 1) for i in range(section_total)]

    def to_sibling(array):
        return lax.ppermute(array, "section", swap)

    def to_replica(array):
        return lax.ppermute(array, "rep", [(0, 1), (1, 0)])

    o_sib, v_sib = to_sibling(o_own), to_sibling(v_own)

    def scalars(own, slot):
        return jnp.stack([jnp.asarray(v, jnp.int32) for v in (own, slot, core, tp)])

    def shape(*dims, dtype=BF16):
        return jax.ShapeDtypeStruct(dims, dtype)

    def dma(*dims):
        return pltpu.SemaphoreType.DMA(dims)

    weight_bytes = model * width * 2
    weight_buffer = pltpu.VMEM((tp_total, cut, width), BF16)

    def reduce_slices(parts, base):
        got = lax.all_to_all(parts, "tp", 0, 0, tiled=True)
        count = parts.shape[1]
        return run(
            reduce_kernel,
            (scalars(1, 0), got, base),
            [SMEM, VMEM, ANY],
            shape(count, cut),
            VMEM,
            [pltpu.VMEM((count, cut), BF16), dma(1)],
            got.size * 2,
        )

    def gather_slices(mine):
        spread = jnp.broadcast_to(mine[None], (tp_total,) + mine.shape)
        return lax.all_to_all(spread, "tp", 0, 0, tiled=True)

    def recompute_slot(slot, x, with_parts):
        halves = (shape(tokens, width),) * 2 + (shape(tokens, width, dtype=F32),) * 2
        outs = ((shape(tp_total, rows, cut),) if with_parts else ()) + halves
        out_specs = ((HBM,) if with_parts else ()) + (VMEM,) * 4
        scratch = [pltpu.VMEM((tp_total, rows, cut), BF16), weight_buffer]
        scratch += [pltpu.VMEM((rows, width), BF16), pltpu.VMEM((rows, width), F32), dma(tp_total), dma(tp_total)]
        if with_parts:
            scratch += [weight_buffer, pltpu.VMEM((tp_total, rows, cut), BF16), dma(tp_total), dma(tp_total)]
        operands = (scalars(1, slot), x, v_own) + ((o_own,) if with_parts else ())
        specs = [SMEM, ANY, ANY] + ([ANY] if with_parts else [])
        count = 2 if with_parts else 1
        return run(
            functools.partial(recompute, tp_total, with_parts),
            operands,
            specs,
            outs,
            out_specs,
            scratch,
            count * weight_bytes,
            count * 2 * rows * model * width,
        )

    x_rows = x_pair.reshape(rows, model)
    parts, act_mine_0, act_other_0, slope_mine_0, slope_other_0 = recompute_slot(0, x_rows, True)
    x_other_0 = lax.dynamic_index_in_dim(x_pair, 1 - core, 0, keepdims=False)
    act_sib_0, slope_sib_0, x_sib_0 = to_sibling(act_other_0), to_sibling(slope_other_0), to_sibling(x_other_0)
    x_second = gather_slices(reduce_slices(parts, x_rows))
    act_mine_1, act_other_1, slope_mine_1, slope_other_1 = recompute_slot(1, x_second, False)
    slope_sib_1 = to_sibling(slope_other_1)
    act_sib_1 = to_sibling(act_other_1)
    x_other_1 = lax.dynamic_slice_in_dim(x_second, (1 - core) * tokens, tokens, 1)
    x_sib_1 = to_sibling(x_other_1)
    slopes = (slope_mine_0, slope_mine_1, slope_sib_0, slope_sib_1)

    def along_chips(heads, grads, places):
        count = len(heads)
        table = jnp.stack([jnp.asarray(v, jnp.int32) for v in [chip, core] + places])
        block = shape(count, tokens, width + 2 * cut)
        cuts = run(
            functools.partial(carve_kernel, count),
            (table, *heads, *grads),
            [SMEM] + [ANY] * (2 * count),
            (block,) * chips,
            (HBM,) * chips,
            [dma(chips * count * 3)],
            chips * count * tokens * (width + 2 * cut) * 4,
        )
        got = [cuts[0]]
        for far in range(1, chips):
            back = chips - far
            got.append(
                lax.ppermute(
                    cuts[back], "section", [(i, (i + 2 * back) % section_total) for i in range(section_total)]
                )
            )
        return got

    def to_owners(got, wanted, place_of):
        count = len(wanted)
        entries = [core, rep]
        for n, layer in enumerate(wanted):
            entries += [far_of[layer], place_of(n, layer)]
        table = jnp.stack([jnp.asarray(v, jnp.int32) for v in entries])
        both, alone = shape(count, tokens, width + piece), shape(count, tokens, piece)
        own_out, own_here, sib_out, sib_here = run(
            functools.partial(pick_kernel, count),
            (table, *got),
            [SMEM] + [ANY] * chips,
            (both, alone, both, alone),
            (HBM,) * 4,
            [dma(count, 6)],
            count * tokens * (width + piece) * 12,
        )
        from_sib, here_sib = to_sibling(sib_out), to_sibling(sib_here)
        return (own_here, own_out, here_sib, from_sib, to_replica(own_out), to_replica(from_sib))

    forward_got = along_chips(
        (act_mine_0, act_mine_1, act_sib_0, act_sib_1),
        (x_pair, x_second, x_sib_0, x_sib_1),
        [2 * core, 2 * core + 1, 2 - 2 * core, 3 - 2 * core],
    )

    down = [(i, i - 2) for i in range(2, section_total)]

    def one_layer(layer, g, deps):
        last = layer == 0
        own = my_map[layer] % 2 == core
        operands = (scalars(own, my_slot[layer]), g, *slopes, o_own, o_sib) + (() if last else (v_own, v_sib))
        outs = (() if last else (shape(tp_total, tokens, cut),)) + (shape(tokens, width),)
        scratch = [pltpu.VMEM((tp_total, tokens, cut), BF16), pltpu.VMEM((1, tokens, width), F32), weight_buffer]
        scratch += [pltpu.VMEM((tokens, width), BF16), dma(tp_total), dma(1), dma(tp_total), dma(1)]
        if not last:
            scratch += [weight_buffer, pltpu.VMEM((tp_total, tokens, cut), BF16), dma(tp_total), dma(tp_total)]
        count = 1 if last else 2
        return run(
            functools.partial(step, tp_total, not last, len(deps)),
            operands + tuple(deps),
            [SMEM] + [ANY] * (len(operands) + len(deps) - 1),
            outs,
            (HBM,) * len(outs),
            scratch,
            count * weight_bytes,
            count * 2 * tokens * model * width,
        )

    g = top_pair
    g_at, head_at = [None] * layers, [None] * layers
    deps = {layer: () for layer in range(layers)}
    upper, middle = list(range(layers - 1, 2, -1)), [2, 1]
    for layer in reversed(range(layers)):
        g_at[layer] = g
        if layer == 5:
            deps[5] = forward_got
            forward = to_owners(
                forward_got, list(range(layers)), lambda n, layer: 2 * (my_map[layer] % 2) + my_slot[layer]
            )
            deps[3] = forward
        if layer == 1:
            deps[1] = upper_got
            upper_all = to_owners(upper_got, upper[::-1], lambda n, layer: n)
            deps[0] = upper_all
        if layer == 0:
            deps[0] = tuple(deps[0]) + tuple(middle_got)
            (head_at[0],) = one_layer(0, g, deps[0])
            break
        parts, head_at[layer] = one_layer(layer, g, deps[layer])
        if layer == upper[-1]:
            order = upper[::-1]
            upper_got = along_chips([head_at[l] for l in order], [g_at[l] for l in order], list(range(len(order))))
        if layer == middle[-1]:
            order = middle[::-1]
            middle_got = along_chips([head_at[l] for l in order], [g_at[l] for l in order], list(range(len(order))))
        mine = reduce_slices(parts, g)
        distance = (section_map[:, layer] // 2) - (section_map[:, layer - 1] // 2)
        my_distance = my_chip[layer] - my_chip[layer - 1]

        def hop(i, value, my_distance=my_distance):
            came = lax.ppermute(value, "section", down)
            return jnp.where(i < my_distance, came, value)

        mine = lax.fori_loop(0, jnp.max(distance), hop, mine)
        g = gather_slices(mine)

    last_got = along_chips([head_at[0]], [g_at[0]], [0])
    middle_all = to_owners(middle_got, middle[::-1], lambda n, layer: n)
    last_all = to_owners(last_got, [0], lambda n, layer: n)
    result = gradients(layers, upper[-1], len(upper), forward, upper_all, None)
    result = gradients(layers, middle[-1], len(middle), forward, middle_all, result)
    return gradients(layers, 0, 1, forward, last_all, result)


def solution(mesh):
    placed = (
        P(),
        P("rep", "section", None, None, None),
        P("rep", None, None, None),
        P("rep", "section", None, "tp"),
        P("rep", "section", None, "tp"),
    )
    return jax.shard_map(
        per_device,
        mesh=mesh,
        in_specs=placed,
        out_specs=(P(None, ("rep", "section"), "tp"), P(None, ("rep", "section"), "tp")),
        check_vma=False,
    )
```

time: 2070 us -> 614 us (0.30)
  waiting for transfers between devices: 1650 us -> 175 us
  Pallas kernels: 0 us -> 195 us
  matrix products: 166 us -> 0 us
  other arithmetic: 79.4 us -> 15.1 us
  starting transfers between devices: 77.7 us -> 128 us
    psum x19 -> x0, waiting for transfers between devices: 1350 us -> none  [add_heads(): summed = lax.psum(term.astype(jnp.bfloat16), 'tp').astype(jnp.float32)]
    pallas_call x0 -> x29, Pallas kernels: none -> 195 us  [the longest x26 186 us: run(): pl.pallas_call(kernel, out_shape=outs, in_specs=specs, out_specs=out_spec...]
    dot_general x44 -> x0, matrix products: 166 us -> none  [the longest x18 75.3 us: one_turn(): jnp.dot(upstream, out_weight[0, slot_index], preferred_element_type=jnp.f...]
    all_to_all x1 -> x16, waiting for transfers between devices: 224 us -> 65 us  [the longest x8 41.5 us: reduce_slices(): got = lax.all_to_all(parts, 'tp', 0, 0, tiled=True)]
    all_to_all x1 -> x16, starting transfers between devices: 6.33 us -> 74.4 us  [the longest x8 39.3 us: reduce_slices(): got = lax.all_to_all(parts, 'tp', 0, 0, tiled=True)]
    scatter x18 -> x0, other arithmetic: 46.9 us -> none  [one_turn(): grad_store.at[slot_index, micro_index]]
    ppermute x9 -> x41, waiting for transfers between devices: 73.2 us -> 110 us  [the longest x5 77.8 us: hop(): came = lax.ppermute(value, 'section', down)]
    unnamed x25 -> x134, local copies, waits for them, and re-layouts: 8.32 us -> 37.7 us
  transfers between devices with their start and end apart: 29 -> 57, of which waited for: 29 -> 20; matrix products, arithmetic and copies ran while one was open for 1% -> 5% of each run, Pallas kernels for 0% -> 26%
where the time goes in v2:
time: 614 us
  Pallas kernels  195 us (32%)
  waiting for transfers between devices  175 us (29%)
  starting transfers between devices  128 us (21%)
  local copies, waits for them, and re-layouts  63.5 us (10%)
  between operations  29.5 us (5%)
  other arithmetic  15.1 us (2%)
  loops' own time  7.81 us (1%)
    pallas_call x26, Pallas kernels, run(): pl.pallas_call(kernel, out_shape=outs, in_specs=specs, out_specs=out_spec...  186 us
    ppermute x5, waiting for transfers between devices, hop(): came = lax.ppermute(value, 'section', down)  77.8 us
    all_to_all x8, waiting for transfers between devices, reduce_slices(): got = lax.all_to_all(parts, 'tp', 0, 0, tiled=True)  41.5 us
    all_to_all x8, starting transfers between devices, reduce_slices(): got = lax.all_to_all(parts, 'tp', 0, 0, tiled=True)  39.3 us
    unnamed x134, local copies, waits for them, and re-layouts  37.7 us
    all_to_all x8, starting transfers between devices, gather_slices(): return lax.all_to_all(spread, 'tp', 0, 0, tiled=True)  35.1 us
    all_to_all x8, waiting for transfers between devices, gather_slices(): return lax.all_to_all(spread, 'tp', 0, 0, tiled=True)  23.4 us
    ppermute x16, starting transfers between devices, to_sibling(): return lax.ppermute(array, 'section', swap)  20.1 us
  transfers between devices with their start and end apart: 57, of which 20 were waited for; matrix products, arithmetic and copies ran while one was open for 5% of the time, Pallas kernels for 26%

profile of v2, /device:TPU:1, one launch (start us, length us, event | category | flops | bytes accessed | tf_op | source)
XLA Modules:
  0.0 613.6 jit_solution(5059707779981030482)
XLA Ops:
  3.5 8.3 %shard_map.68 = (bf16[8,128,512]{2,1,0:T(8,128)(2,1)}, bf16[64,512]{1,0:T(8,128)(2,1)S(1)}, bf16[64,512]{1,0:T(8,128)(2,1)S(1)}, f32[64,512]{1,0:T(8,128)S(1)}, f32[64,512]{1,0:T(8,128)}) custom-call(s32[4]{0:T(128)S(1)} %add_add_fusion.scalars, bf16[128,4096]{1,0:T(8,128)(2,1)S(1)} %bitcast.71, bf16[2,4096,512]{2,1,0:T(8,128)(2,1)} %bitcast.78, ...), custom_call_target="tpu_custom_call" | custom-call | flops 1073741824 | bytes 8388608 | tf_op jit(solution)/shard_map/pallas_call | solution.py:27
  18.4 14.9 %all-to-all-done.got_ref = bf16[8,128,512]{2,1,0:T(8,128)(2,1)S(1)} async-done(((bf16[8,128,512]{2,1,0:T(8,128)(2,1)}), bf16[8,128,512]{2,1,0:T(8,128)(2,1)S(1)}, u32[]{:S(2)}, u32[]{:S(2)}) %all-to-all-start) | async-done | bytes 1048608 | tf_op jit(solution)/shard_map/all_to_all | solution.py:317
  42.9 10.4 %all-to-all-done.1.x_ref.refs_5_ = bf16[8,128,512]{2,1,0:T(8,128)(2,1)S(1)} async-done(((bf16[8,128,512]{2,1,0:T(8,128)(2,1)}), bf16[8,128,512]{2,1,0:T(8,128)(2,1)S(1)}, u32[]{:S(2)}, u32[]{:S(2)}) %all-to-all-start.1) | async-done | bytes 1048608 | tf_op jit(solution)/shard_map/all_to_all | solution.py:331
  78.6 7.5 %all-to-all-done.2.got_ref = bf16[8,64,512]{2,1,0:T(8,128)(2,1)} async-done(((bf16[8,64,512]{2,1,0:T(8,128)(2,1)}), bf16[8,64,512]{2,1,0:T(8,128)(2,1)}, u32[]{:S(2)}, u32[]{:S(2)}) %all-to-all-start.2) | async-done | bytes 524320 | tf_op jit(solution)/shard_map/all_to_all | solution.py:317
  87.9 8.1 %while.70 = (s32[]{:T(128)}, bf16[64,512]{1,0:T(8,128)(2,1)}, s32[]{:T(128)}, s32[]{:T(128)}, s32[]{:T(128)}) while((s32[]{:T(128)}, bf16[64,512]{1,0:T(8,128)(2,1)}, s32[]{:T(128)}, s32[]{:T(128)}, s32[]{:T(128)}) %tuple.151), condition=%wide.region_3.4_spmd, body=%wide.region_2.3_spmd.sunk | while | flops 32771 | bytes 458871 | solution.py:473
  108.4 6.9 %shard_map.75 = (bf16[8,64,512]{2,1,0:T(8,128)(2,1)}, bf16[64,512]{1,0:T(8,128)(2,1)S(1)}) custom-call(s32[4]{0:T(128)S(1)} %add_add_fusion.8.scalars, bf16[8,64,512]{2,1,0:T(8,128)(2,1)S(1)} %all-to-all-done.3.g_ref.base_ref.refs_8_, f32[64,512]{1,0:T(8,128)S(1)} %get-tuple-element.235.refs_0_, f32[64,512]{1,0:T(8,128)S(1)} %get-tuple-element.236.refs_1_, ...), custom_call_target="tpu_custom_call" | custom-call | flops 536870912 | bytes 8388608 | tf_op jit(solution)/shard_map/pallas_call | solution.py:27
  126.7 37.9 %shard_map.71 = (bf16[4,64,1536]{2,1,0:T(8,128)(2,1)S(1)}, bf16[4,64,1536]{2,1,0:T(8,128)(2,1)}, bf16[4,64,1536]{2,1,0:T(8,128)(2,1)}, bf16[4,64,1536]{2,1,0:T(8,128)(2,1)}) custom-call(s32[6]{0:T(128)S(1)} %stack.222.scalars, bf16[64,512]{1,0:T(8,128)(2,1)S(1)} %copy-done.42, bf16[64,512]{1,0:T(8,128)(2,1)S(1)} %copy-done.44, ...), custom_call_target="tpu_custom_call" | custom-call | bytes 6291456 | tf_op jit(solution)/shard_map/pallas_call | solution.py:27
  169.0 33.6 %while.71 = (s32[]{:T(128)}, bf16[64,512]{1,0:T(8,128)(2,1)S(1)}, s32[]{:T(128)}, s32[]{:T(128)}, s32[]{:T(128)}) while((s32[]{:T(128)}, bf16[64,512]{1,0:T(8,128)(2,1)S(1)}, s32[]{:T(128)}, s32[]{:T(128)}, s32[]{:T(128)}) %tuple.154), condition=%wide.region_6.7_spmd, body=%wide.region_5.6_spmd.sunk | while | flops 32771 | bytes 458871 | solution.py:473
  171.2 30.8 %collective-permute-done.1 = bf16[64,512]{1,0:T(8,128)(2,1)S(1)} collective-permute-done((bf16[64,512]{1,0:T(8,128)(2,1)S(1)}, bf16[64,512]{1,0:T(8,128)(2,1)S(1)}, u32[]{:S(2)}, u32[]{:S(2)}) %collective-permute-start.1) | collective-permute-done | bytes 65568 | tf_op jit(solution)/shard_map/while/body/ppermute | solution.py:470
  216.8 6.9 %shard_map.77 = (bf16[8,64,512]{2,1,0:T(8,128)(2,1)}, bf16[64,512]{1,0:T(8,128)(2,1)S(1)}) custom-call(s32[4]{0:T(128)S(1)} %add_add_fusion.7.scalars, bf16[8,64,512]{2,1,0:T(8,128)(2,1)S(1)} %all-to-all-done.5.g_ref.base_ref.refs_7_, f32[64,512]{1,0:T(8,128)S(1)} %get-tuple-element.235.refs_0_, f32[64,512]{1,0:T(8,128)S(1)} %get-tuple-element.236.refs_1_, ...), custom_call_target="tpu_custom_call" | custom-call | flops 536870912 | bytes 8388608 | tf_op jit(solution)/shard_map/pallas_call | solution.py:27
  230.0 6.7 %all-to-all-done.6.got_ref = bf16[8,64,512]{2,1,0:T(8,128)(2,1)S(1)} async-done(((bf16[8,64,512]{2,1,0:T(8,128)(2,1)}), bf16[8,64,512]{2,1,0:T(8,128)(2,1)S(1)}, u32[]{:S(2)}, u32[]{:S(2)}) %all-to-all-start.6) | async-done | bytes 524320 | tf_op jit(solution)/shard_map/all_to_all | solution.py:317
  268.7 6.9 %shard_map.79 = (bf16[8,64,512]{2,1,0:T(8,128)(2,1)}, bf16[64,512]{1,0:T(8,128)(2,1)S(1)}) custom-call(s32[4]{0:T(128)S(1)} %add_add_fusion.6.scalars, bf16[8,64,512]{2,1,0:T(8,128)(2,1)S(1)} %all-to-all-done.7.g_ref.base_ref.refs_6_, f32[64,512]{1,0:T(8,128)S(1)} %get-tuple-element.235.refs_0_, f32[64,512]{1,0:T(8,128)S(1)} %get-tuple-element.236.refs_1_, ...), custom_call_target="tpu_custom_call" | custom-call | flops 536870912 | bytes 8388608 | tf_op jit(solution)/shard_map/pallas_call | solution.py:27
  293.9 8.1 %while.73 = (s32[]{:T(128)}, bf16[64,512]{1,0:T(8,128)(2,1)}, s32[]{:T(128)}, s32[]{:T(128)}, s32[]{:T(128)}) while((s32[]{:T(128)}, bf16[64,512]{1,0:T(8,128)(2,1)}, s32[]{:T(128)}, s32[]{:T(128)}, s32[]{:T(128)}) %tuple.160), condition=%wide.region_12.13_spmd, body=%wide.region_11.12_spmd.sunk | while | flops 32771 | bytes 458871 | solution.py:473
  311.5 18.9 %collective-permute-done.17.refs_13_.refs_5_ = bf16[8,64,768]{2,1,0:T(8,128)(2,1)S(1)} collective-permute-done((bf16[8,64,768]{2,1,0:T(8,128)(2,1)S(1)}, bf16[8,64,768]{2,1,0:T(8,128)(2,1)S(1)}, u32[]{:S(2)}, u32[]{:S(2)}) %collective-permute-start.17) | collective-permute-done | bytes 786464 | tf_op jit(solution)/shard_map/ppermute | solution.py:300
  331.6 6.9 %shard_map.81 = (bf16[8,64,512]{2,1,0:T(8,128)(2,1)S(1)}, bf16[64,512]{1,0:T(8,128)(2,1)S(1)}) custom-call(s32[4]{0:T(128)S(1)} %add_add_fusion.5.scalars, bf16[8,64,512]{2,1,0:T(8,128)(2,1)} %all-to-all-done.9.g_ref.base_ref.refs_5_, f32[64,512]{1,0:T(8,128)S(1)} %get-tuple-element.235.refs_0_, f32[64,512]{1,0:T(8,128)S(1)} %get-tuple-element.236.refs_1_, ...), custom_call_target="tpu_custom_call" | custom-call | flops 536870912 | bytes 8388608 | tf_op jit(solution)/shard_map/pallas_call | solution.py:27
  345.7 8.5 %all-to-all-done.10.got_ref = bf16[8,64,512]{2,1,0:T(8,128)(2,1)} async-done(((bf16[8,64,512]{2,1,0:T(8,128)(2,1)}), bf16[8,64,512]{2,1,0:T(8,128)(2,1)}, u32[]{:S(2)}, u32[]{:S(2)}) %all-to-all-start.10) | async-done | bytes 524320 | tf_op jit(solution)/shard_map/all_to_all | solution.py:317
  356.7 8.1 %while.74 = (s32[]{:T(128)}, bf16[64,512]{1,0:T(8,128)(2,1)}, s32[]{:T(128)}, s32[]{:T(128)}, s32[]{:T(128)}) while((s32[]{:T(128)}, bf16[64,512]{1,0:T(8,128)(2,1)}, s32[]{:T(128)}, s32[]{:T(128)}, s32[]{:T(128)}) %tuple.163), condition=%wide.region_15.16_spmd, body=%wide.region_14.15_spmd.sunk | while | flops 32771 | bytes 458871 | solution.py:473
  371.4 6.4 %all-to-all-done.11.g_ref.base_ref.refs_3_ = bf16[8,64,512]{2,1,0:T(8,128)(2,1)} async-done(((bf16[8,64,512]{2,1,0:T(8,128)(2,1)}), bf16[8,64,512]{2,1,0:T(8,128)(2,1)}, u32[]{:S(2)}, u32[]{:S(2)}) %all-to-all-start.11) | async-done | bytes 524320 | tf_op jit(solution)/shard_map/all_to_all | solution.py:331
  399.1 26.2 %shard_map.85 = (bf16[5,64,1536]{2,1,0:T(8,128)(2,1)S(1)}, bf16[5,64,1536]{2,1,0:T(8,128)(2,1)}, bf16[5,64,1536]{2,1,0:T(8,128)(2,1)}, bf16[5,64,1536]{2,1,0:T(8,128)(2,1)}) custom-call(s32[7]{0:T(128)S(1)} %stack.252.scalars, bf16[64,512]{1,0:T(8,128)(2,1)S(1)} %copy-done.50, bf16[64,512]{1,0:T(8,128)(2,1)S(1)} %copy-done.46, ...), custom_call_target="tpu_custom_call" | custom-call | bytes 7864320 | tf_op jit(solution)/shard_map/pallas_call | solution.py:27
  432.3 38.8 %while.75 = (s32[]{:T(128)}, bf16[64,512]{1,0:T(8,128)(2,1)}, s32[]{:T(128)}, s32[]{:T(128)}, s32[]{:T(128)}) while((s32[]{:T(128)}, bf16[64,512]{1,0:T(8,128)(2,1)}, s32[]{:T(128)}, s32[]{:T(128)}, s32[]{:T(128)}) %tuple.166), condition=%wide.region_18.19_spmd, body=%wide.region_17.18_spmd.sunk | while | flops 32771 | bytes 458871 | solution.py:473
  434.2 34.8 %collective-permute-done.5 = bf16[64,512]{1,0:T(8,128)(2,1)} collective-permute-done((bf16[64,512]{1,0:T(8,128)(2,1)}, bf16[64,512]{1,0:T(8,128)(2,1)}, u32[]{:S(2)}, u32[]{:S(2)}) %collective-permute-start.5) | collective-permute-done | bytes 65568 | tf_op jit(solution)/shard_map/while/body/ppermute | solution.py:470
  482.9 16.8 %shard_map.88 = (bf16[5,64,768]{2,1,0:T(8,128)(2,1)S(1)}, bf16[5,64,256]{2,1,0:T(8,128)(2,1)S(1)}, bf16[5,64,768]{2,1,0:T(8,128)(2,1)}, bf16[5,64,256]{2,1,0:T(8,128)(2,1)S(1)}) custom-call(s32[12]{0:T(128)S(1)} %stack.253.scalars, bf16[5,64,1536]{2,1,0:T(8,128)(2,1)S(1)} %copy-done.15, bf16[5,64,1536]{2,1,0:T(8,128)(2,1)} %collective-permute-done.22.refs_9_.refs_1_, ...), custom_call_target="tpu_custom_call" | custom-call | bytes 2949120 | tf_op jit(solution)/shard_map/pallas_call | solution.py:27
  507.8 6.9 %shard_map.86 = (bf16[8,64,512]{2,1,0:T(8,128)(2,1)S(1)}, bf16[64,512]{1,0:T(8,128)(2,1)S(1)}) custom-call(s32[4]{0:T(128)S(1)} %add_add_fusion.3.scalars, bf16[8,64,512]{2,1,0:T(8,128)(2,1)} %all-to-all-done.13.g_ref.base_ref.refs_2_, f32[64,512]{1,0:T(8,128)S(1)} %get-tuple-element.235.refs_0_, f32[64,512]{1,0:T(8,128)S(1)} %get-tuple-element.236.refs_1_, ...), custom_call_target="tpu_custom_call" | custom-call | flops 536870912 | bytes 8388608 | tf_op jit(solution)/shard_map/pallas_call | solution.py:27
  525.0 17.8 %shard_map.89 = (bf16[2,64,1536]{2,1,0:T(8,128)(2,1)S(1)}, bf16[2,64,1536]{2,1,0:T(8,128)(2,1)S(1)}, bf16[2,64,1536]{2,1,0:T(8,128)(2,1)}, bf16[2,64,1536]{2,1,0:T(8,128)(2,1)}) custom-call(s32[4]{0:T(128)S(1)} %pad_add_fusion.2.scalars, bf16[64,512]{1,0:T(8,128)(2,1)S(1)} %copy-done.56, bf16[64,512]{1,0:T(8,128)(2,1)S(1)} %copy-done.48, ...), custom_call_target="tpu_custom_call" | custom-call | bytes 3145728 | tf_op jit(solution)/shard_map/pallas_call | solution.py:27
  (305 shorter events, 297.0 us)
Async XLA Ops:
  0.6 63.9 %collective-permute-start.21 = (bf16[2,4096,512]{2,1,0:T(8,128)(2,1)}, bf16[2,4096,512]{2,1,0:T(8,128)(2,1)}, u32[]{:S(2)}, u32[]{:S(2)}) collective-permute-start(bf16[2,4096,512]{2,1,0:T(8,128)(2,1)} %bitcast.77), channel_id=1, source_target_pairs={{0,8},{8,0},{16,24},{24,16},{32,40},{40,32},{48,56},{56,48},{1,9},... | collective-permute-start | bytes 25165832 | tf_op jit(solution)/shard_map/ppermute | solution.py:297
  2.1 62.4 %collective-permute-start.20 = (bf16[2,4096,512]{2,1,0:T(8,128)(2,1)}, bf16[2,4096,512]{2,1,0:T(8,128)(2,1)}, u32[]{:S(2)}, u32[]{:S(2)}) collective-permute-start(bf16[2,4096,512]{2,1,0:T(8,128)(2,1)} %bitcast.87), channel_id=1, source_target_pairs={{0,8},{8,0},{16,24},{24,16},{32,40},{40,32},{48,56},{56,48},{1,9},... | collective-permute-start | bytes 25165832 | tf_op jit(solution)/shard_map/ppermute | solution.py:297
  17.7 46.8 %collective-permute-start.18 = (f32[64,512]{1,0:T(8,128)}, f32[64,512]{1,0:T(8,128)S(1)}, u32[]{:S(2)}, u32[]{:S(2)}) collective-permute-start(f32[64,512]{1,0:T(8,128)} %get-tuple-element.237), channel_id=1, source_target_pairs={{0,8},{8,0},{16,24},{24,16},{32,40},{40,32},{48,56},{56,48},{1,9},... | collective-permute-start | bytes 393224 | tf_op jit(solution)/shard_map/ppermute | solution.py:297
  102.1 22.3 %collective-permute-start.9 = (bf16[64,4096]{1,0:T(8,128)(2,1)}, bf16[64,4096]{1,0:T(8,128)(2,1)}, u32[]{:S(2)}, u32[]{:S(2)}) collective-permute-start(bf16[64,4096]{1,0:T(8,128)(2,1)} %dynamic-slice_bitcast_fusion), channel_id=1, source_target_pairs={{0,8},{8,0},{16,24},{24,16},{32,40},{40,32},{48,56},{56,48},{1,9},... | collective-permute-start | bytes 1572872 | tf_op jit(solution)/shard_map/ppermute | solution.py:297
  115.3 53.0 %all-to-all-start.4 = ((bf16[8,64,512]{2,1,0:T(8,128)(2,1)}), bf16[8,64,512]{2,1,0:T(8,128)(2,1)S(1)}, u32[]{:S(2)}, u32[]{:S(2)}) async-start(bf16[8,64,512]{2,1,0:T(8,128)(2,1)} %get-tuple-element.241), calls=%async_computation.4 | async-start | bytes 1048576 | tf_op jit(solution)/shard_map/all_to_all | solution.py:317
  164.7 46.5 %collective-permute-start.11 = (bf16[4,64,1536]{2,1,0:T(8,128)(2,1)}, bf16[4,64,1536]{2,1,0:T(8,128)(2,1)}, u32[]{:S(2)}, u32[]{:S(2)}) collective-permute-start(bf16[4,64,1536]{2,1,0:T(8,128)(2,1)} %get-tuple-element.228), channel_id=1, source_target_pairs={{0,48},{8,56},{16,0},{24,8},{32,16},{40,24},{48,32},{56,40},{1,49}... | collective-permute-start | bytes 2359304 | tf_op jit(solution)/shard_map/ppermute | solution.py:384
  165.8 45.3 %collective-permute-start.12 = (bf16[4,64,1536]{2,1,0:T(8,128)(2,1)}, bf16[4,64,1536]{2,1,0:T(8,128)(2,1)}, u32[]{:S(2)}, u32[]{:S(2)}) collective-permute-start(bf16[4,64,1536]{2,1,0:T(8,128)(2,1)} %get-tuple-element.229), channel_id=1, source_target_pairs={{0,32},{8,40},{16,48},{24,56},{32,0},{40,8},{48,16},{56,24},{1,33}... | collective-permute-start | bytes 2359304 | tf_op jit(solution)/shard_map/ppermute | solution.py:384
  167.7 43.4 %collective-permute-start.13 = (bf16[4,64,1536]{2,1,0:T(8,128)(2,1)}, bf16[4,64,1536]{2,1,0:T(8,128)(2,1)}, u32[]{:S(2)}, u32[]{:S(2)}) collective-permute-start(bf16[4,64,1536]{2,1,0:T(8,128)(2,1)} %get-tuple-element.230), channel_id=1, source_target_pairs={{0,16},{8,24},{16,32},{24,40},{32,48},{40,56},{48,0},{56,8},{1,17}... | collective-permute-start | bytes 2359304 | tf_op jit(solution)/shard_map/ppermute | solution.py:384
  169.9 32.1 %collective-permute-start.1 = (bf16[64,512]{1,0:T(8,128)(2,1)S(1)}, bf16[64,512]{1,0:T(8,128)(2,1)S(1)}, u32[]{:S(2)}, u32[]{:S(2)}) collective-permute-start(bf16[64,512]{1,0:T(8,128)(2,1)S(1)} %get-tuple-element.609), channel_id=1, source_target_pairs={{16,0},{24,8},{32,16},{40,24},{48,32},{56,40},{17,1},{25,9},{33,17... | collective-permute-start | bytes 196616 | tf_op jit(solution)/shard_map/while/body/ppermute | solution.py:470
  239.0 29.7 %all-to-all-start.7 = ((bf16[8,64,512]{2,1,0:T(8,128)(2,1)}), bf16[8,64,512]{2,1,0:T(8,128)(2,1)S(1)}, u32[]{:S(2)}, u32[]{:S(2)}) async-start(bf16[8,64,512]{2,1,0:T(8,128)(2,1)} %broadcast_in_dim.19), calls=%async_computation.7 | async-start | bytes 1048576 | tf_op jit(solution)/shard_map/all_to_all | solution.py:331
  282.7 28.8 %collective-permute-start.16 = (bf16[8,64,768]{2,1,0:T(8,128)(2,1)S(1)}, bf16[8,64,768]{2,1,0:T(8,128)(2,1)S(1)}, u32[]{:S(2)}, u32[]{:S(2)}) collective-permute-start(bf16[8,64,768]{2,1,0:T(8,128)(2,1)S(1)} %get-tuple-element.232.refs_9_.refs_1_), channel_id=1, source_target_pairs={{0,64},{64,0},{1,65},{65,1},{2,66},{66,2},{3,67},{67,3},{4,68},{68... | collective-permute-start | bytes 2359304 | tf_op jit(solution)/shard_map/ppermute | solution.py:300
  287.0 43.4 %collective-permute-start.17 = (bf16[8,64,768]{2,1,0:T(8,128)(2,1)S(1)}, bf16[8,64,768]{2,1,0:T(8,128)(2,1)S(1)}, u32[]{:S(2)}, u32[]{:S(2)}) collective-permute-start(bf16[8,64,768]{2,1,0:T(8,128)(2,1)S(1)} %collective-permute-done.15.refs_11_.refs_3_), channel_id=1, source_target_pairs={{0,64},{64,0},{1,65},{65,1},{2,66},{66,2},{3,67},{67,3},{4,68},{68... | collective-permute-start | bytes 2359304 | tf_op jit(solution)/shard_map/ppermute | solution.py:300
  303.7 26.9 %all-to-all-start.9 = ((bf16[8,64,512]{2,1,0:T(8,128)(2,1)}), bf16[8,64,512]{2,1,0:T(8,128)(2,1)}, u32[]{:S(2)}, u32[]{:S(2)}) async-start(bf16[8,64,512]{2,1,0:T(8,128)(2,1)} %broadcast_in_dim.20), calls=%async_computation.9 | async-start | bytes 1048576 | tf_op jit(solution)/shard_map/all_to_all | solution.py:331
  385.6 44.1 %all-to-all-start.12 = ((bf16[8,64,512]{2,1,0:T(8,128)(2,1)}), bf16[8,64,512]{2,1,0:T(8,128)(2,1)}, u32[]{:S(2)}, u32[]{:S(2)}) async-start(bf16[8,64,512]{2,1,0:T(8,128)(2,1)} %copy-done.27), calls=%async_computation.12 | async-start | bytes 1048576 | tf_op jit(solution)/shard_map/all_to_all | solution.py:317
  426.2 55.4 %collective-permute-start.22 = (bf16[5,64,1536]{2,1,0:T(8,128)(2,1)}, bf16[5,64,1536]{2,1,0:T(8,128)(2,1)}, u32[]{:S(2)}, u32[]{:S(2)}) collective-permute-start(bf16[5,64,1536]{2,1,0:T(8,128)(2,1)} %get-tuple-element.257), channel_id=1, source_target_pairs={{0,48},{8,56},{16,0},{24,8},{32,16},{40,24},{48,32},{56,40},{1,49}... | collective-permute-start | bytes 2949128 | tf_op jit(solution)/shard_map/ppermute | solution.py:384
  427.7 54.0 %collective-permute-start.23 = (bf16[5,64,1536]{2,1,0:T(8,128)(2,1)}, bf16[5,64,1536]{2,1,0:T(8,128)(2,1)}, u32[]{:S(2)}, u32[]{:S(2)}) collective-permute-start(bf16[5,64,1536]{2,1,0:T(8,128)(2,1)} %get-tuple-element.258), channel_id=1, source_target_pairs={{0,32},{8,40},{16,48},{24,56},{32,0},{40,8},{48,16},{56,24},{1,33}... | collective-permute-start | bytes 2949128 | tf_op jit(solution)/shard_map/ppermute | solution.py:384
  429.2 52.5 %collective-permute-start.24 = (bf16[5,64,1536]{2,1,0:T(8,128)(2,1)}, bf16[5,64,1536]{2,1,0:T(8,128)(2,1)}, u32[]{:S(2)}, u32[]{:S(2)}) collective-permute-start(bf16[5,64,1536]{2,1,0:T(8,128)(2,1)} %get-tuple-element.259), channel_id=1, source_target_pairs={{0,16},{8,24},{16,32},{24,40},{32,48},{40,56},{48,0},{56,8},{1,17}... | collective-permute-start | bytes 2949128 | tf_op jit(solution)/shard_map/ppermute | solution.py:384
  432.8 36.1 %collective-permute-start.5 = (bf16[64,512]{1,0:T(8,128)(2,1)}, bf16[64,512]{1,0:T(8,128)(2,1)}, u32[]{:S(2)}, u32[]{:S(2)}) collective-permute-start(bf16[64,512]{1,0:T(8,128)(2,1)} %get-tuple-element.669), channel_id=1, source_target_pairs={{16,0},{24,8},{32,16},{40,24},{48,32},{56,40},{17,1},{25,9},{33,17... | collective-permute-start | bytes 196616 | tf_op jit(solution)/shard_map/while/body/ppermute | solution.py:470
  472.8 33.8 %all-to-all-start.13 = ((bf16[8,64,512]{2,1,0:T(8,128)(2,1)}), bf16[8,64,512]{2,1,0:T(8,128)(2,1)}, u32[]{:S(2)}, u32[]{:S(2)}) async-start(bf16[8,64,512]{2,1,0:T(8,128)(2,1)} %broadcast_in_dim.22), calls=%async_computation.13 | async-start | bytes 1048576 | tf_op jit(solution)/shard_map/all_to_all | solution.py:331
  501.8 46.5 %collective-permute-start.26 = (bf16[5,64,768]{2,1,0:T(8,128)(2,1)}, bf16[5,64,768]{2,1,0:T(8,128)(2,1)}, u32[]{:S(2)}, u32[]{:S(2)}) collective-permute-start(bf16[5,64,768]{2,1,0:T(8,128)(2,1)} %get-tuple-element.265), channel_id=1, source_target_pairs={{0,8},{8,0},{16,24},{24,16},{32,40},{40,32},{48,56},{56,48},{1,9},... | collective-permute-start | bytes 1474568 | tf_op jit(solution)/shard_map/ppermute | solution.py:297
  516.1 29.2 %all-to-all-start.14 = ((bf16[8,64,512]{2,1,0:T(8,128)(2,1)}), bf16[8,64,512]{2,1,0:T(8,128)(2,1)}, u32[]{:S(2)}, u32[]{:S(2)}) async-start(bf16[8,64,512]{2,1,0:T(8,128)(2,1)} %copy-done.28), calls=%async_computation.14 | async-start | bytes 1048576 | tf_op jit(solution)/shard_map/all_to_all | solution.py:317
  522.8 51.8 %collective-permute-start.27 = (bf16[5,64,768]{2,1,0:T(8,128)(2,1)}, bf16[5,64,768]{2,1,0:T(8,128)(2,1)}, u32[]{:S(2)}, u32[]{:S(2)}) collective-permute-start(bf16[5,64,768]{2,1,0:T(8,128)(2,1)} %copy-done.19), channel_id=1, source_target_pairs={{0,64},{64,0},{1,65},{65,1},{2,66},{66,2},{3,67},{67,3},{4,68},{68... | collective-permute-start | bytes 1474568 | tf_op jit(solution)/shard_map/ppermute | solution.py:300
  549.0 25.6 %collective-permute-start.28 = (bf16[5,64,768]{2,1,0:T(8,128)(2,1)}, bf16[5,64,768]{2,1,0:T(8,128)(2,1)}, u32[]{:S(2)}, u32[]{:S(2)}) collective-permute-start(bf16[5,64,768]{2,1,0:T(8,128)(2,1)} %collective-permute-done.26.refs_9_), channel_id=1, source_target_pairs={{0,64},{64,0},{1,65},{65,1},{2,66},{66,2},{3,67},{67,3},{4,68},{68... | collective-permute-start | bytes 1474568 | tf_op jit(solution)/shard_map/ppermute | solution.py:300
  587.5 21.9 %collective-permute-start.41 = (bf16[2,64,768]{2,1,0:T(8,128)(2,1)S(1)}, bf16[2,64,768]{2,1,0:T(8,128)(2,1)S(1)}, u32[]{:S(2)}, u32[]{:S(2)}) collective-permute-start(bf16[2,64,768]{2,1,0:T(8,128)(2,1)S(1)} %copy-done.32), channel_id=1, source_target_pairs={{0,64},{64,0},{1,65},{65,1},{2,66},{66,2},{3,67},{67,3},{4,68},{68... | collective-permute-start | bytes 589832 | tf_op jit(solution)/shard_map/ppermute | solution.py:300
  (100 other events, 881.0 us)
